TPU v7x, 32 devices: a whole 2x2x4 slice. The times are simulated.
32 devices in a mesh: expert: 16 (over z, x, core), fsdp: 2 (over y).
Axes of the slice: x: 2, y: 2, z: 4, core: 2. Of those that a mesh axis runs over, the one named last changes fastest.
Arguments:
- tokens: bfloat16 [2, 2048, 2048], P('fsdp', 'expert'), may hold values from -6 to 6
- routes: int32 [2, 2048, 6], P('fsdp', 'expert'), may hold values from 0 to 15, all different within a row; in each aligned block of 128 rows (0 to 127, 128 to 255, ..., all dimensions but the last counted through in order) at most 64 rows name the same one
- cotangent: bfloat16 [2, 2048, 2048], P('fsdp', 'expert'), may hold values from -6 to 6
- attn_gain: bfloat16 [2048], P('fsdp'), may hold values from 0.5 to 1.5
- w_query: bfloat16 [2048, 3072], P('fsdp'), may hold values from -0.3125 to 0.3125
- latent_weight: bfloat16 [2048, 576], P('fsdp'), may hold values from -0.125 to 0.125
- latent_norm_gain: bfloat16 [512], P('fsdp'), may hold values from 0.5 to 1.5
- expand_weight: bfloat16 [512, 4096], P('fsdp'), may hold values from -0.25 to 0.25
- w_out: bfloat16 [2048, 2048], P('fsdp'), may hold values from -0.25 to 0.25
- ffn_gain: bfloat16 [2048], P('fsdp'), may hold values from 0.5 to 1.5
- w_router: bfloat16 [2048, 16], P('fsdp'), may hold values from -0.0625 to 0.0625
- shared_gate: bfloat16 [2048, 2816], P(('expert', 'fsdp')), may hold values from -0.125 to 0.125
- shared_up: bfloat16 [2048, 2816], P(('expert', 'fsdp')), may hold values from -0.125 to 0.125
- shared_down: bfloat16 [2816, 2048], P(('expert', 'fsdp')), may hold values from -0.15625 to 0.15625
- expert_gate: bfloat16 [16, 2048, 1408], P('expert', None, 'fsdp'), may hold values from -0.125 to 0.125
- expert_up: bfloat16 [16, 2048, 1408], P('expert', None, 'fsdp'), may hold values from -0.125 to 0.125
- expert_down: bfloat16 [16, 1408, 2048], P('expert', 'fsdp'), may hold values from -3 to 3
Outputs:
- output: bfloat16 [2, 2048, 2048], P('fsdp', 'expert')
- tokens_grad: bfloat16 [2, 2048, 2048], P('fsdp', 'expert')
- attn_gain_grad: float32 [2048], P('fsdp')
- w_query_grad: float32 [2048, 3072], P('fsdp')
- w_latent_grad: float32 [2048, 576], P('fsdp')
- latent_gain_grad: float32 [512], P('fsdp')
- w_expand_grad: float32 [512, 4096], P('fsdp')
- w_out_grad: float32 [2048, 2048], P('fsdp')
- ffn_gain_grad: float32 [2048], P('fsdp')
- w_router_grad: float32 [2048, 16], P('fsdp')
- shared_gate_grad: float32 [2048, 2816], P(('expert', 'fsdp'))
- shared_up_grad: float32 [2048, 2816], P(('expert', 'fsdp'))
- shared_down_grad: float32 [2816, 2048], P(('expert', 'fsdp'))
- expert_gate_grad: float32 [16, 2048, 1408], P('expert', None, 'fsdp')
- expert_up_grad: float32 [16, 2048, 1408], P('expert', None, 'fsdp')
- expert_down_grad: float32 [16, 1408, 2048], P('expert', 'fsdp')
Inputs may be any that keep to these rules, and one draw needn't show every extreme that they name: `routes`: in each aligned block of 128 rows (the rows of one device), no expert is named by more than 64 routed pairs, a bound that some block reaches; a token names 6 different experts.
All inputs are finite; a program needn't handle non-finite values.
Results may differ from a plain program's by a relative error of at most 0.03.
Values may be sent and summed in bfloat16 or wider, within the bound.
A program may use at most 512 MiB of HBM per device.

v0:
```python
import functools

import jax
import jax.numpy as jnp
import numpy as np
from jax import lax
from jax.experimental import pallas as pl
from jax.experimental.pallas import tpu as pltpu
from jax.sharding import PartitionSpec as P

MODEL_WIDTH = 2048
HEAD_COUNT = 16
PLAIN_UNITS = 128
ROTARY_UNITS = 64
VALUE_UNITS = 128
LATENT_WIDTH = 512
TOPK = 6


EPS = 1e-06


def matrix_product(left, right):
    return jnp.dot(left, right, preferred_element_type=jnp.float32)


def inner(left, right):
    return lax.dot_general(
        left, right, (((0,), (0,)), ((), ())), preferred_element_type=jnp.float32
    )


def outer_product(left, right):
    return lax.dot_general(
        left, right, (((1,), (1,)), ((), ())), preferred_element_type=jnp.float32
    )


def norm_forward(value, gain):
    inverse = lax.rsqrt(jnp.mean(value * value, axis=-1, keepdims=True) + EPS)
    return (value * inverse * gain, inverse)


def norm_backward(value, inverse, gain, grad):
    unit = value * inverse
    scaled = grad * gain
    d_value = inverse * (scaled - unit * jnp.mean(scaled * unit, axis=-1, keepdims=True))
    return (d_value, jnp.sum(grad * unit, axis=0))


def rope_tables(positions):
    half = ROTARY_UNITS // 2
    freqs = 10000.0 ** (-jnp.arange(half, dtype=jnp.float32) * (2.0 / ROTARY_UNITS))
    angles = positions.astype(jnp.float32)[:, None] * freqs[None, :]
    return (jnp.cos(angles), jnp.sin(angles))


def apply_rotary(value, cosine_table, sine_table):
    half = ROTARY_UNITS // 2
    first = value[..., :half]
    second = value[..., half:]
    return jnp.concatenate(
        [first * cosine_table - second * sine_table, first * sine_table + second * cosine_table],
        axis=-1,
    )


def reverse_rotary(grad, cosine_table, sine_table):
    half = ROTARY_UNITS // 2
    first = grad[..., :half]
    second = grad[..., half:]
    return jnp.concatenate(
        [first * cosine_table + second * sine_table, second * cosine_table - first * sine_table],
        axis=-1,
    )


def silu_parts(value):
    sigma = jax.nn.sigmoid(value)
    return (value * sigma, sigma * (1.0 + value * (1.0 - sigma)))


def body(
    tokens,
    routes,
    cotangent,
    attn_gain,
    w_query,
    latent_weight,
    latent_norm_gain,
    expand_weight,
    w_out,
    ffn_gain,
    w_router,
    shared_gate,
    shared_up,
    shared_down,
    expert_gate,
    expert_up,
    expert_down,
):
    device_local = tokens.shape[1]
    experts = lax.axis_size("expert")
    shards = lax.axis_size("fsdp")
    position = lax.axis_index("expert")
    capacity = shards * (
        (device_local * TOPK * 4 + experts * 3 * shards - 1) // (experts * 3 * shards)
    )
    seq_len = device_local * experts
    feature_width = LATENT_WIDTH + ROTARY_UNITS
    scale = (PLAIN_UNITS + ROTARY_UNITS) ** (-0.5)
    attention_gain_grad, wq, wlat, g_lat, expand_matrix, wout, g_ffn, wrout = (
        lax.all_gather(attn_gain, "fsdp", axis=0, tiled=True),
        lax.all_gather(w_query, "fsdp", axis=0, tiled=True),
        lax.all_gather(latent_weight, "fsdp", axis=0, tiled=True),
        lax.all_gather(latent_norm_gain, "fsdp", axis=0, tiled=True),
        lax.all_gather(expand_weight, "fsdp", axis=0, tiled=True),
        lax.all_gather(w_out, "fsdp", axis=0, tiled=True),
        lax.all_gather(ffn_gain, "fsdp", axis=0, tiled=True),
        lax.all_gather(w_router, "fsdp", axis=0, tiled=True),
    )
    sgate, sup, sdown = (
        lax.all_gather(shared_gate, ("expert", "fsdp"), axis=0, tiled=True),
        lax.all_gather(shared_up, ("expert", "fsdp"), axis=0, tiled=True),
        lax.all_gather(shared_down, ("expert", "fsdp"), axis=0, tiled=True),
    )
    attention_gain_grad = attention_gain_grad.astype(jnp.float32)
    g_lat = g_lat.astype(jnp.float32)
    g_ffn = g_ffn.astype(jnp.float32)
    x_in = tokens[0].astype(jnp.float32)
    grad_out = cotangent[0].astype(jnp.float32)
    positions = position * device_local + jnp.arange(device_local, dtype=jnp.int32)
    cosine_table, sine_table = rope_tables(positions)
    normed, inv_attn = norm_forward(x_in, attention_gain_grad)
    normed_in = normed.astype(jnp.bfloat16)
    query_full = matrix_product(normed_in, wq).reshape(
        device_local, HEAD_COUNT, PLAIN_UNITS + ROTARY_UNITS
    )
    query_nope = query_full[:, :, :PLAIN_UNITS].astype(jnp.bfloat16)
    expanded_latent = expand_matrix.reshape(LATENT_WIDTH, HEAD_COUNT, PLAIN_UNITS + VALUE_UNITS)
    key_part = expanded_latent[:, :, :PLAIN_UNITS]
    value_part = expanded_latent[:, :, PLAIN_UNITS:]
    query_latent = jnp.einsum(
        "thd,chd->thc", query_nope, key_part, preferred_element_type=jnp.float32
    )
    query_rope = apply_rotary(
        query_full[:, :, PLAIN_UNITS:], cosine_table[:, None, :], sine_table[:, None, :]
    )
    token_rows = device_local * HEAD_COUNT
    query = (
        jnp.concatenate([query_latent, query_rope], axis=-1)
        .astype(jnp.bfloat16)
        .reshape(token_rows, feature_width)
    )
    latent_complete = matrix_product(normed_in, wlat)
    packed_rows = latent_complete[:, :LATENT_WIDTH]
    latent_state, inv_lat = norm_forward(packed_rows, g_lat)
    rotary_key = apply_rotary(latent_complete[:, LATENT_WIDTH:], cosine_table, sine_table)
    key = jnp.concatenate([latent_state, rotary_key], axis=-1).astype(jnp.bfloat16)
    keys_all = lax.all_gather(key, "expert", axis=0, tiled=True)
    block = min(512, seq_len)
    token_tally = (position * device_local + device_local + block - 1) // block
    q_pos = position * device_local + jnp.arange(token_rows, dtype=jnp.int32) // HEAD_COUNT

    def scores_of(index):
        key_rows = lax.dynamic_slice_in_dim(keys_all, index * block, block, 0)
        raw = outer_product(query, key_rows)
        k_pos = index * block + jnp.arange(block, dtype=jnp.int32)
        valid = k_pos[None, :] <= q_pos[:, None]
        return (jnp.where(valid, raw * scale, -1e30), key_rows)

    def stats_step(index, carry):
        top, total = carry
        scores, unused = scores_of(index)
        new_top = jnp.maximum(top, jnp.max(scores, axis=1))
        total = total * jnp.exp(top - new_top) + jnp.sum(jnp.exp(scores - new_top[:, None]), axis=1)
        return (new_top, total)

    top, total = lax.fori_loop(
        0,
        token_tally,
        stats_step,
        (jnp.full((token_rows,), -1e30, jnp.float32), jnp.zeros((token_rows,), jnp.float32)),
    )
    log_total = top + jnp.log(total)

    def mixing_update(index, running_total):
        scores, key_rows = scores_of(index)
        weight_arrays = jnp.exp(scores - log_total[:, None]).astype(jnp.bfloat16)
        return running_total + matrix_product(weight_arrays, key_rows[:, :LATENT_WIDTH])

    mixed_output_sum = lax.fori_loop(
        0, token_tally, mixing_update, jnp.zeros((token_rows, LATENT_WIDTH), jnp.float32)
    )
    mixed_output = mixed_output_sum.astype(jnp.bfloat16).reshape(
        device_local, HEAD_COUNT, LATENT_WIDTH
    )
    heads = jnp.einsum("thc,chv->thv", mixed_output, value_part, preferred_element_type=jnp.float32)
    heads = heads.reshape(device_local, HEAD_COUNT * VALUE_UNITS).astype(jnp.bfloat16)
    hidden = x_in + matrix_product(heads, wout)
    normed2, inv_ffn = norm_forward(hidden, g_ffn)
    normed_ffn = normed2.astype(jnp.bfloat16)
    logits = matrix_product(normed_ffn, wrout)
    router = jax.nn.softmax(logits, axis=-1)
    own_routes = routes[0]
    names = jnp.arange(experts, dtype=jnp.int32)
    chosen = (own_routes[:, :, None] == names[None, None, :]).astype(jnp.float32)
    gates = jnp.sum(chosen * router[:, None, :], axis=-1)
    hits = (own_routes.reshape(device_local * TOPK)[:, None] == names[None, :]).astype(jnp.int32)
    slot = jnp.sum((jnp.cumsum(hits, axis=0) - hits) * hits, axis=1)
    place = own_routes.reshape(device_local * TOPK) * capacity + slot
    token_of = jnp.arange(device_local * TOPK, dtype=jnp.int32) // TOPK
    table = jnp.full((experts * capacity,), device_local, jnp.int32).at[place].set(token_of)
    padded = jnp.concatenate([normed_ffn, jnp.zeros((1, MODEL_WIDTH), jnp.bfloat16)], axis=0)
    buffer = padded[table].reshape(experts, capacity, MODEL_WIDTH)
    w_g, w_u, w_d = (expert_gate[0], expert_up[0], expert_down[0])

    def spread(values):
        return jnp.broadcast_to(values[:, None], (experts, shards, capacity, MODEL_WIDTH)).reshape(
            experts * shards, capacity, MODEL_WIDTH
        )

    def collect(back):
        return jnp.sum(back.reshape(experts, shards, capacity, MODEL_WIDTH), axis=1).reshape(
            experts * capacity, MODEL_WIDTH
        )

    received = lax.all_to_all(
        spread(buffer), ("expert", "fsdp"), split_axis=0, concat_axis=0, tiled=True
    )
    ex_rows = received.reshape(-1, MODEL_WIDTH)
    pre_gate = matrix_product(ex_rows, w_g)
    pre_up = matrix_product(ex_rows, w_u)
    act_gate, slope = silu_parts(pre_gate)
    ex_act = (act_gate * pre_up).astype(jnp.bfloat16)
    ex_out = matrix_product(ex_act, w_d).reshape(received.shape)
    returned = lax.all_to_all(
        ex_out.astype(jnp.bfloat16), ("expert", "fsdp"), split_axis=0, concat_axis=0, tiled=True
    ).astype(ex_out.dtype)
    results = collect(returned)
    picked = results[place].reshape(device_local, TOPK, MODEL_WIDTH)
    routed = jnp.sum(gates[:, :, None] * picked, axis=1)
    sh_gate = matrix_product(normed_ffn, sgate)
    sh_up = matrix_product(normed_ffn, sup)
    sh_silu, sh_slope = silu_parts(sh_gate)
    sh_act = (sh_silu * sh_up).astype(jnp.bfloat16)
    shared = matrix_product(sh_act, sdown)
    output = hidden + routed + shared
    d_shared = grad_out.astype(jnp.bfloat16)
    shared_down_gradient = inner(sh_act, d_shared)
    d_sh_act = outer_product(d_shared, sdown)
    d_sh_gate = (d_sh_act * sh_up * sh_slope).astype(jnp.bfloat16)
    d_sh_up = (d_sh_act * sh_silu).astype(jnp.bfloat16)
    shared_gate_gradient = inner(normed_ffn, d_sh_gate)
    shared_up_gradient = inner(normed_ffn, d_sh_up)
    d_normed_ffn = outer_product(d_sh_gate, sgate) + outer_product(d_sh_up, sup)
    d_picked = (
        (gates[:, :, None] * grad_out[:, None, :])
        .astype(jnp.bfloat16)
        .reshape(device_local * TOPK, MODEL_WIDTH)
    )
    d_gates = jnp.sum(picked * grad_out[:, None, :], axis=2)
    d_buffer = (
        jnp.zeros((experts * capacity, MODEL_WIDTH), jnp.bfloat16)
        .at[place]
        .set(d_picked)
        .reshape(experts, capacity, MODEL_WIDTH)
    )
    d_received = lax.all_to_all(
        spread(d_buffer), ("expert", "fsdp"), split_axis=0, concat_axis=0, tiled=True
    )
    d_rows = d_received.reshape(-1, MODEL_WIDTH)
    d_act = outer_product(d_rows, w_d)
    g_down = inner(ex_act, d_rows)
    d_pre_gate = (d_act * pre_up * slope).astype(jnp.bfloat16)
    d_pre_up = (d_act * act_gate).astype(jnp.bfloat16)
    g_gate = inner(ex_rows, d_pre_gate)
    g_up = inner(ex_rows, d_pre_up)
    d_ex_rows = (outer_product(d_pre_gate, w_g) + outer_product(d_pre_up, w_u)).reshape(
        received.shape
    )
    d_returned = lax.all_to_all(
        d_ex_rows.astype(jnp.bfloat16), ("expert", "fsdp"), split_axis=0, concat_axis=0, tiled=True
    ).astype(d_ex_rows.dtype)
    d_results = collect(d_returned)
    d_normed_ffn = d_normed_ffn + jnp.sum(
        d_results[place].reshape(device_local, TOPK, MODEL_WIDTH), axis=1
    )
    d_router = jnp.sum(chosen * d_gates[:, :, None], axis=1)
    d_logits = (router * (d_router - jnp.sum(router * d_router, axis=1, keepdims=True))).astype(
        jnp.bfloat16
    )
    router_weight_gradient = inner(normed_ffn, d_logits)
    d_normed_ffn = d_normed_ffn + outer_product(d_logits, wrout)
    d_hidden_norm, g_ffn_grad = norm_backward(hidden, inv_ffn, g_ffn, d_normed_ffn)
    d_hidden = grad_out + d_hidden_norm
    d_attn = d_hidden.astype(jnp.bfloat16)
    output_weight_gradient = inner(heads, d_attn)
    d_heads = (
        outer_product(d_attn, wout)
        .astype(jnp.bfloat16)
        .reshape(device_local, HEAD_COUNT, VALUE_UNITS)
    )
    value_weight_gradient = jnp.einsum(
        "thc,thv->chv", mixed_output, d_heads, preferred_element_type=jnp.float32
    )
    mixed_gradient = jnp.einsum(
        "thv,chv->thc", d_heads, value_part, preferred_element_type=jnp.float32
    )
    mixed_gradient = mixed_gradient.astype(jnp.bfloat16).reshape(token_rows, LATENT_WIDTH)
    delta = jnp.sum(mixed_gradient.astype(jnp.float32) * mixed_output_sum, axis=1)

    def back_step(index, carry):
        d_query_acc, d_keys_acc = carry
        scores, key_rows = scores_of(index)
        weight_arrays = jnp.exp(scores - log_total[:, None])
        weight_gradients = outer_product(mixed_gradient, key_rows[:, :LATENT_WIDTH])
        d_scores = (weight_arrays * (weight_gradients - delta[:, None]) * scale).astype(
            jnp.bfloat16
        )
        d_query_acc = d_query_acc + matrix_product(d_scores, key_rows)
        d_values = inner(weight_arrays.astype(jnp.bfloat16), mixed_gradient)
        d_block = inner(d_scores, query) + jnp.concatenate(
            [d_values, jnp.zeros((block, ROTARY_UNITS), jnp.float32)], axis=1
        )
        previous = lax.dynamic_slice_in_dim(d_keys_acc, index * block, block, 0)
        return (
            d_query_acc,
            lax.dynamic_update_slice_in_dim(d_keys_acc, previous + d_block, index * block, 0),
        )

    d_query, d_keys = lax.fori_loop(
        0,
        token_tally,
        back_step,
        (
            jnp.zeros((token_rows, feature_width), jnp.float32),
            jnp.zeros((seq_len, feature_width), jnp.float32),
        ),
    )
    key_gradient = lax.psum_scatter(
        d_keys.astype(jnp.bfloat16), "expert", scatter_dimension=0, tiled=True
    )
    query_up_gradient = d_query.astype(jnp.bfloat16).reshape(
        device_local, HEAD_COUNT, feature_width
    )
    query_latent_gradient = query_up_gradient[:, :, :LATENT_WIDTH]
    key_weight_gradient = jnp.einsum(
        "thc,thd->chd", query_latent_gradient, query_nope, preferred_element_type=jnp.float32
    )
    d_q_nope = jnp.einsum(
        "thc,chd->thd", query_latent_gradient, key_part, preferred_element_type=jnp.float32
    )
    d_q_rope = reverse_rotary(
        query_up_gradient[:, :, LATENT_WIDTH:].astype(jnp.float32),
        cosine_table[:, None, :],
        sine_table[:, None, :],
    )
    d_query_full = (
        jnp.concatenate([d_q_nope, d_q_rope], axis=-1)
        .astype(jnp.bfloat16)
        .reshape(device_local, HEAD_COUNT * (PLAIN_UNITS + ROTARY_UNITS))
    )
    query_weight_gradient = inner(normed_in, d_query_full)
    d_normed_in = outer_product(d_query_full, wq)
    latent_gradient = key_gradient[:, :LATENT_WIDTH].astype(jnp.float32)
    rotary_key_gradient = reverse_rotary(
        key_gradient[:, LATENT_WIDTH:].astype(jnp.float32), cosine_table, sine_table
    )
    d_compact, g_lat_grad = norm_backward(packed_rows, inv_lat, g_lat, latent_gradient)
    d_latent_full = jnp.concatenate([d_compact, rotary_key_gradient], axis=-1).astype(jnp.bfloat16)
    latent_weight_gradient = inner(normed_in, d_latent_full)
    d_normed_in = d_normed_in + outer_product(d_latent_full, wlat)
    d_norm_in, g_attn_grad = norm_backward(x_in, inv_attn, attention_gain_grad, d_normed_in)
    d_tokens = (d_hidden + d_norm_in).astype(jnp.bfloat16)
    expand_weight_gradient = jnp.concatenate(
        [key_weight_gradient, value_weight_gradient], axis=-1
    ).reshape(LATENT_WIDTH, HEAD_COUNT * (PLAIN_UNITS + VALUE_UNITS))
    r_sgate, r_sup, r_sdown = (
        lax.psum_scatter(shared_gate_gradient, ("expert", "fsdp"), scatter_dimension=0, tiled=True),
        lax.psum_scatter(shared_up_gradient, ("expert", "fsdp"), scatter_dimension=0, tiled=True),
        lax.psum_scatter(shared_down_gradient, ("expert", "fsdp"), scatter_dimension=0, tiled=True),
    )
    r_attn, r_query, r_latent, r_lgain, r_expand, r_out, r_fgain, r_router = (
        lax.psum_scatter(
            g_attn_grad.astype(jnp.bfloat16), "fsdp", scatter_dimension=0, tiled=True
        ).astype(jnp.float32),
        lax.psum_scatter(
            query_weight_gradient.astype(jnp.bfloat16), "fsdp", scatter_dimension=0, tiled=True
        ).astype(jnp.float32),
        lax.psum_scatter(
            latent_weight_gradient.astype(jnp.bfloat16), "fsdp", scatter_dimension=0, tiled=True
        ).astype(jnp.float32),
        lax.psum_scatter(
            g_lat_grad.astype(jnp.bfloat16), "fsdp", scatter_dimension=0, tiled=True
        ).astype(jnp.float32),
        lax.psum_scatter(
            expand_weight_gradient.astype(jnp.bfloat16), "fsdp", scatter_dimension=0, tiled=True
        ).astype(jnp.float32),
        lax.psum_scatter(
            output_weight_gradient.astype(jnp.bfloat16), "fsdp", scatter_dimension=0, tiled=True
        ).astype(jnp.float32),
        lax.psum_scatter(
            g_ffn_grad.astype(jnp.bfloat16), "fsdp", scatter_dimension=0, tiled=True
        ).astype(jnp.float32),
        lax.psum_scatter(
            router_weight_gradient.astype(jnp.bfloat16), "fsdp", scatter_dimension=0, tiled=True
        ).astype(jnp.float32),
    )
    r_attn, r_query, r_latent, r_lgain, r_expand, r_out, r_fgain, r_router = (
        lax.psum(r_attn.astype(jnp.bfloat16), "expert").astype(jnp.float32),
        lax.psum(r_query.astype(jnp.bfloat16), "expert").astype(jnp.float32),
        lax.psum(r_latent.astype(jnp.bfloat16), "expert").astype(jnp.float32),
        lax.psum(r_lgain.astype(jnp.bfloat16), "expert").astype(jnp.float32),
        lax.psum(r_expand.astype(jnp.bfloat16), "expert").astype(jnp.float32),
        lax.psum(r_out.astype(jnp.bfloat16), "expert").astype(jnp.float32),
        lax.psum(r_fgain.astype(jnp.bfloat16), "expert").astype(jnp.float32),
        lax.psum(r_router.astype(jnp.bfloat16), "expert").astype(jnp.float32),
    )
    return (
        output.astype(jnp.bfloat16)[None],
        d_tokens[None],
        r_attn,
        r_query,
        r_latent,
        r_lgain,
        r_expand,
        r_out,
        r_fgain,
        r_router,
        r_sgate,
        r_sup,
        r_sdown,
        g_gate[None],
        g_up[None],
        g_down[None],
    )


LINE = 4
SQUARE = 2
CORES = 2
MESH = pl.DeviceIdType.MESH
VMEM_LIMIT = 56 * 1024 * 1024


class Place:
    def __init__(self):
        index = lax.axis_index("expert")
        self.y = lax.axis_index("fsdp")
        self.c = lax.rem(index, CORES)
        self.b = lax.rem(lax.div(index, CORES), SQUARE)
        self.a = lax.div(index, CORES * SQUARE)

    def device(self, da=0, db=0, dc=0, dy=0):
        b = 1 - self.b if db else self.b
        c = 1 - self.c if dc else self.c
        y = 1 - self.y if dy else self.y
        return (((self.a + da) * SQUARE + b) * CORES + c, y)

    def block(self, full, a, db=0, dc=0, dy=0):
        b = 1 - self.b if db else self.b
        c = 1 - self.c if dc else self.c
        y = 1 - self.y if dy else self.y
        flat = (a * SQUARE + b) * CORES + c
        return y * (LINE * SQUARE * CORES) + flat if full else flat

    def greet(self, with_y):
        barrier = pltpu.get_barrier_semaphore()
        near = [dict(db=1), dict(dc=1)] + ([dict(dy=1)] if with_y else [])
        for step in near:
            pl.semaphore_signal(barrier, inc=1, device_id=self.device(**step), device_id_type=MESH)

        @pl.when(self.a > 0)
        def _():
            pl.semaphore_signal(barrier, inc=1, device_id=self.device(da=-1), device_id_type=MESH)

        @pl.when(self.a < LINE - 1)
        def _():
            pl.semaphore_signal(barrier, inc=1, device_id=self.device(da=1), device_id_type=MESH)

        ends = jnp.logical_or(self.a == 0, self.a == LINE - 1).astype(jnp.int32)
        pl.semaphore_wait(barrier, len(near) + 2 - ends)


class Sender:
    def __init__(self, place, sems):
        self.place, self.sems, self.pending = place, sems, []

    def send(self, src, dst, recv_sem, step, cond=None):
        sem = self.sems.at[len(self.pending)]

        def make():
            return pltpu.make_async_remote_copy(
                src_ref=src,
                dst_ref=dst,
                send_sem=sem,
                recv_sem=recv_sem,
                device_id=self.place.device(**step),
                device_id_type=MESH,
            )

        def start():
            make().start()

        guarded(cond, start)
        self.pending.append((cond, lambda: make().wait_send()))

    def arrived(self, dst, recv_sem):
        pltpu.make_async_remote_copy(
            src_ref=dst,
            dst_ref=dst,
            send_sem=self.sems.at[0],
            recv_sem=recv_sem,
            device_id=self.place.device(dc=1),
            device_id_type=MESH,
        ).wait_recv()

    def finish(self):
        for cond, wait in self.pending:
            guarded(cond, wait)


def guarded(cond, action):
    if cond is None:
        action()
    else:
        pl.when(cond)(action)


def both(first, second):
    if first is None or second is None:
        return second if first is None else first
    return jnp.logical_and(first, second)


def gather_ticks(place, sender, full, gated, ins, outs, local_sems, recv_sems):
    a = place.a
    count = len(ins)

    def own_copy(at):
        return pltpu.make_async_copy(
            ins[at], outs[at].at[place.block(full, a)], local_sems.at[at]
        )

    def chunk(at, block, half):
        size = ins[at].shape[0] // 2
        return outs[at].at[block, pl.ds(half * size, size)]

    def sem_of(at, block, half):
        return recv_sems.at[at, block * 2 + half]

    def forward(at, block, half, src, step, cond=None):
        sender.send(src, chunk(at, block, half), sem_of(at, block, half), step, cond)

    def receive(at, block, half, cond):
        guarded(cond, lambda: sender.arrived(chunk(at, block, half), sem_of(at, block, half)))

    def held_by(at, delta, cond):
        if at not in gated:
            return cond
        return both(cond, lax.div(a + delta, LINE // 2) == place.y)

    def from_line(delta, always):
        for half in range(2):
            for at in range(count):
                block = place.block(full, a + delta)
                cond = held_by(at, delta, always)
                size = ins[at].shape[0] // 2
                if delta == 0:
                    src = ins[at].at[pl.ds(half * size, size)]
                else:
                    receive(at, block, half, cond)
                    src = chunk(at, block, half)
                if delta <= 0:
                    forward(at, block, half, src, dict(da=1), both(cond, a < LINE - 1))
                if delta >= 0:
                    forward(at, block, half, src, dict(da=-1), both(cond, a > 0))
                forward(at, block, half, src, dict(db=1), cond)
                if full:
                    forward(at, block, half, src, dict(dy=1), cond)
                forward(at, block, half, src, dict(dc=1), cond)

    def from_side(delta, always):
        for half in range(2):
            for at in range(count):
                cond = held_by(at, delta, always)
                block = place.block(full, a + delta, db=1)
                receive(at, block, half, cond)
                if full and half == 0:
                    forward(at, block, half, chunk(at, block, half), dict(dy=1), cond)
                forward(at, block, half, chunk(at, block, half), dict(dc=1), cond)
                if full:
                    block = place.block(full, a + delta, dy=1)
                    receive(at, block, half, cond)
                    if half == 1:
                        forward(at, block, half, chunk(at, block, half), dict(db=1), cond)
                    forward(at, block, half, chunk(at, block, half), dict(dc=1), cond)

    def from_corner(delta, always):
        for half in range(2):
            for at in range(count):
                cond = held_by(at, delta, always)
                block = place.block(True, a + delta, db=1, dy=1)
                receive(at, block, half, cond)
                forward(at, block, half, chunk(at, block, half), dict(dc=1), cond)

    def from_sibling(delta, always):
        for half in range(2):
            for at in range(count):
                cond = held_by(at, delta, always)
                for db in range(2):
                    for dy in range(2 if full else 1):
                        receive(at, place.block(full, a + delta, db=db, dc=1, dy=dy), half, cond)

    rounds = [[(0, None)]]
    for s in range(1, LINE):
        rounds.append([(-s, a >= s), (s, a + s < LINE)])
    stages = [from_line, from_side] + ([from_corner] if full else []) + [from_sibling]

    def tick(number):
        if number == 0:
            for at in range(count):
                own_copy(at).start()
        for level, stage in enumerate(stages):
            if 0 <= number - level < len(rounds):
                for delta, cond in rounds[number - level]:
                    stage(delta, cond)
        if number == len(rounds) + len(stages) - 2:
            for at in range(count):
                own_copy(at).wait()

    return [functools.partial(tick, number) for number in range(len(rounds) + len(stages) - 1)]


def send_pairs(sender, ins, outs, sems):
    for at, (src, dst) in enumerate(zip(ins, outs)):
        sender.send(src, dst, sems.at[at], dict(dy=1))


def take_pairs(sender, outs, sems):
    for at, dst in enumerate(outs):
        sender.arrived(dst, sems.at[at])


def gather_kernel(full, count, pairs, halved, gated, *refs):
    arrays = count + pairs + halved
    ins, outs = refs[:arrays], refs[arrays : 2 * arrays]
    local_sems, send_sems, recv_sems, pair_sems, half_sems = refs[2 * arrays :]
    place = Place()
    sender = Sender(place, send_sems)
    place.greet(full or pairs + halved > 0)
    shared = range(count + pairs, arrays)

    def part(ref, core):
        size = ref.shape[0] // CORES
        return ref.at[pl.ds(pl.multiple_of(core * size, 16), size)]

    send_pairs(sender, ins[count : count + pairs], outs[count : count + pairs], pair_sems)
    for at in shared:
        sender.send(
            part(ins[at], place.c), part(outs[at], place.c), half_sems.at[at - count - pairs, 0],
            dict(dy=1),
        )
    ticks = gather_ticks(
        place, sender, full, gated, ins[:count], outs[:count], local_sems, recv_sems
    )
    for number, tick in enumerate(ticks):
        if number == len(ticks) - 1:
            for at in shared:
                here = part(outs[at], place.c)
                sender.arrived(here, half_sems.at[at - count - pairs, 0])
                sender.send(here, here, half_sems.at[at - count - pairs, 1], dict(dc=1))
        tick()
    for at in shared:
        sender.arrived(part(outs[at], 1 - place.c), half_sems.at[at - count - pairs, 1])
    take_pairs(sender, outs[count : count + pairs], pair_sems)
    sender.finish()


def gather_rows(arrays, full, collective_id, swapped=(), halved=(), gated=()):
    blocks = LINE * SQUARE * CORES * (SQUARE if full else 1)
    count, pairs, shared = len(arrays), len(swapped), len(halved)
    lines = 2 * LINE - 1
    sends = pairs + 2 * shared + count * lines * 2 * (9 if full else 5)
    moved = sum(blocks * 2 * x.size * x.dtype.itemsize for x in arrays)
    return pl.pallas_call(
        functools.partial(gather_kernel, full, count, pairs, shared, gated),
        out_shape=[jax.ShapeDtypeStruct((blocks,) + x.shape, x.dtype) for x in arrays]
        + [jax.ShapeDtypeStruct(x.shape, x.dtype) for x in (*swapped, *halved)],
        in_specs=[pl.BlockSpec(memory_space=pl.ANY)] * (count + pairs + shared),
        out_specs=[pl.BlockSpec(memory_space=pl.ANY)] * (count + pairs + shared),
        scratch_shapes=[
            pltpu.SemaphoreType.DMA((count,)),
            pltpu.SemaphoreType.DMA((sends,)),
            pltpu.SemaphoreType.DMA((count, blocks * 2)),
            pltpu.SemaphoreType.DMA((max(pairs, 1),)),
            pltpu.SemaphoreType.DMA((max(shared, 1), 2)),
        ],
        compiler_params=pltpu.CompilerParams(collective_id=collective_id, has_side_effects=True),
        cost_estimate=pl.CostEstimate(flops=0, bytes_accessed=6 * moved, transcendentals=0),
    )(*arrays, *swapped, *halved)


def add_rows(target, sources, size):
    def step(at, carry):
        rows = pl.ds(pl.multiple_of(at * 16, 16), 16)
        total = sources[0][rows, :].astype(jnp.float32)
        for source in sources[1:]:
            total = total + source[rows, :].astype(jnp.float32)
        target[rows, :] = total.astype(target.dtype)
        return carry

    lax.fori_loop(0, size // 16, step, 0)


def scatter_ticks(place, sender, full, part, out, scratch):
    mine, got, side, up, down, load_sems, recv_sems = scratch
    a = place.a
    kinds = 4 if full else 2
    size = part.shape[1]
    half = size // 2
    order = [LINE - 1, 0, LINE - 2, 1]
    walk = (3, 1, 2, 0) if full else (1, 0)

    def sem_of(group, target, kind):
        return recv_sems.at[group, target * 4 + kind]

    def load(target, kind):
        block = place.block(full, target, db=kind % 2, dy=kind // 2)
        return pltpu.make_async_copy(
            part.at[block], mine.at[target, kind], load_sems.at[target * 4 + kind]
        )

    def begin():
        for target in order:
            for kind in walk:
                load(target, kind).start()
                block = place.block(full, target, db=kind % 2, dc=1, dy=kind // 2)
                sender.send(
                    part.at[block], got.at[target, kind], sem_of(0, target, kind), dict(dc=1)
                )

    def rows_of(ref, which):
        return ref.at[pl.ds(which * half, half)]

    def over_cores(target):
        for kind in walk:
            load(target, kind).wait()
            sender.arrived(got.at[target, kind], sem_of(0, target, kind))
            add_rows(mine.at[target, kind], [mine.at[target, kind], got.at[target, kind]], size)
            held = mine.at[target, kind]
            if kind == 3:
                sender.send(rows_of(held, 0), side.at[target, 4], sem_of(1, target, 0), dict(db=1))
                sender.send(rows_of(held, 1), side.at[target, 5], sem_of(1, target, 1), dict(dy=1))
            if kind == 1:
                sender.send(rows_of(held, 0), side.at[target, 0], sem_of(2, target, 0), dict(db=1))
                if not full:
                    sender.send(
                        rows_of(held, 1), side.at[target, 1], sem_of(2, target, 1), dict(db=1)
                    )
            if kind == 2:
                sender.send(rows_of(held, 1), side.at[target, 3], sem_of(2, target, 3), dict(dy=1))

    def over_corner(target):
        sender.arrived(side.at[target, 4], sem_of(1, target, 0))
        held = rows_of(mine.at[target, 2], 0)
        add_rows(held, [held, side.at[target, 4]], half)
        sender.send(held, side.at[target, 2], sem_of(2, target, 2), dict(dy=1))
        sender.arrived(side.at[target, 5], sem_of(1, target, 1))
        held = rows_of(mine.at[target, 1], 1)
        add_rows(held, [held, side.at[target, 5]], half)
        sender.send(held, side.at[target, 1], sem_of(2, target, 1), dict(db=1))

    def gathered(target, which):
        held = rows_of(mine.at[target, 0], which)
        parts = [held]
        for source in (0, 2) if full else (0,):
            sender.arrived(side.at[target, source + which], sem_of(2, target, source + which))
            parts.append(side.at[target, source + which])
        return held, parts

    def line_slots(target, which):
        below, above = rows_of(up.at[target], which), rows_of(down.at[target], which)
        return below, sem_of(3, target, which), above, sem_of(3, target, 2 + which)

    def over_line(target):
        def relay(which, slot, slot_sem, at_end):
            held, parts = gathered(target, which)

            def with_slot():
                sender.arrived(slot, slot_sem)
                add_rows(held, parts + [slot], half)

            pl.when(jnp.logical_not(at_end))(with_slot)
            pl.when(at_end)(lambda: add_rows(held, parts, half))

        for which in range(2):
            below, below_sem, above, above_sem = line_slots(target, which)
            held = rows_of(mine.at[target, 0], which)
            if target > 0:
                pl.when(a < target)(
                    functools.partial(relay, which, below, below_sem, a == 0)
                )
                sender.send(held, below, below_sem, dict(da=1), a < target)
            if target < LINE - 1:
                pl.when(a > target)(
                    functools.partial(relay, which, above, above_sem, a == LINE - 1)
                )
                sender.send(held, above, above_sem, dict(da=-1), a > target)

    def own_total(target):
        for which in range(2):
            below, below_sem, above, above_sem = line_slots(target, which)
            _, parts = gathered(target, which)
            if target > 0:
                sender.arrived(below, below_sem)
                parts.append(below)
            if target < LINE - 1:
                sender.arrived(above, above_sem)
                parts.append(above)
            add_rows(rows_of(out, which), parts, half)

    stages = [over_cores] + ([over_corner] if full else []) + [over_line]

    def tick(number):
        if number == 0:
            begin()
        for level, stage in enumerate(stages):
            if 0 <= number - level < len(order):
                stage(order[number - level])
        if number == len(order) + len(stages) - 2:
            for target in range(LINE):
                pl.when(a == target)(functools.partial(own_total, target))

    return [functools.partial(tick, number) for number in range(len(order) + len(stages) - 1)]


def scatter_kernel(full, pairs, part, *refs):
    ins, out, outs = refs[:pairs], refs[pairs], refs[pairs + 1 : 2 * pairs + 1]
    mine, got, side, up, down, load_sems, send_sems, recv_sems, pair_sems = refs[2 * pairs + 1 :]
    place = Place()
    sender = Sender(place, send_sems)
    place.greet(full or pairs > 0)
    send_pairs(sender, ins, outs, pair_sems)
    scratch = (mine, got, side, up, down, load_sems, recv_sems)
    for tick in scatter_ticks(place, sender, full, part, out, scratch):
        tick()
    take_pairs(sender, outs, pair_sems)
    sender.finish()


def scatter_scratch(full, rows, width, dtype, pairs):
    kinds = 4 if full else 2
    return [
        pltpu.VMEM((LINE, kinds, rows, width), dtype),
        pltpu.VMEM((LINE, kinds, rows, width), dtype),
        pltpu.VMEM((LINE, 6, rows // 2, width), dtype),
        pltpu.VMEM((LINE, rows, width), dtype),
        pltpu.VMEM((LINE, rows, width), dtype),
        pltpu.SemaphoreType.DMA((LINE * 4,)),
        pltpu.SemaphoreType.DMA((pairs + LINE * (4 + 6 + 4),)),
        pltpu.SemaphoreType.DMA((4, LINE * 4)),
        pltpu.SemaphoreType.DMA((max(pairs, 1),)),
    ]


def gather_scatter_kernel(count, gated, *refs):
    ins, part = refs[:count], refs[count]
    outs, total = refs[count + 1 : 2 * count + 1], refs[2 * count + 1]
    local_sems, gather_sends, gather_recvs = refs[2 * count + 2 : 2 * count + 5]
    mine, got, side, up, down, load_sems, scatter_sends, scatter_recvs, _ = refs[2 * count + 5 :]
    place = Place()
    gatherer = Sender(place, gather_sends)
    scatterer = Sender(place, scatter_sends)
    place.greet(True)
    scratch = (mine, got, side, up, down, load_sems, scatter_recvs)
    ticks = [
        scatter_ticks(place, scatterer, True, part, total, scratch),
        gather_ticks(place, gatherer, False, gated, ins, outs, local_sems, gather_recvs),
    ]
    for number in range(max(len(steps) for steps in ticks)):
        for steps in ticks:
            if number < len(steps):
                steps[number]()
    scatterer.finish()
    gatherer.finish()


def gather_and_scatter(arrays, part, collective_id, gated=()):
    blocks = LINE * SQUARE * CORES
    count = len(arrays)
    _, rows, width = part.shape
    sends = count * (2 * LINE - 1) * 2 * 5
    moved = sum(blocks * 2 * x.size * x.dtype.itemsize for x in arrays)
    return pl.pallas_call(
        functools.partial(gather_scatter_kernel, count, gated),
        out_shape=[jax.ShapeDtypeStruct((blocks,) + x.shape, x.dtype) for x in arrays]
        + [jax.ShapeDtypeStruct((rows, width), jnp.float32)],
        in_specs=[pl.BlockSpec(memory_space=pl.ANY)] * (count + 1),
        out_specs=[pl.BlockSpec(memory_space=pl.ANY)] * count
        + [pl.BlockSpec(memory_space=pltpu.VMEM)],
        scratch_shapes=[
            pltpu.SemaphoreType.DMA((count,)),
            pltpu.SemaphoreType.DMA((sends,)),
            pltpu.SemaphoreType.DMA((count, blocks * 2)),
        ]
        + scatter_scratch(True, rows, width, part.dtype, 0),
        compiler_params=pltpu.CompilerParams(
            collective_id=collective_id, has_side_effects=True, vmem_limit_bytes=VMEM_LIMIT
        ),
        cost_estimate=pl.CostEstimate(flops=0, bytes_accessed=6 * moved, transcendentals=0),
    )(*arrays, part)


def scatter_rows(part, full, collective_id, swapped=()):
    blocks, rows, width = part.shape
    pairs = len(swapped)
    return pl.pallas_call(
        functools.partial(scatter_kernel, full, pairs),
        out_shape=[jax.ShapeDtypeStruct((rows, width), jnp.float32)]
        + [jax.ShapeDtypeStruct(x.shape, x.dtype) for x in swapped],
        in_specs=[pl.BlockSpec(memory_space=pl.ANY)] * (1 + pairs),
        out_specs=[pl.BlockSpec(memory_space=pltpu.VMEM)]
        + [pl.BlockSpec(memory_space=pl.ANY)] * pairs,
        scratch_shapes=scatter_scratch(full, rows, width, part.dtype, pairs),
        compiler_params=pltpu.CompilerParams(
            collective_id=collective_id, has_side_effects=True, vmem_limit_bytes=VMEM_LIMIT
        ),
        cost_estimate=pl.CostEstimate(
            flops=0, bytes_accessed=12 * part.size * part.dtype.itemsize, transcendentals=0
        ),
    )(part, *swapped)


def contract_last(left, right):
    return lax.dot_general(
        left, right, (((1,), (1,)), ((), ())), preferred_element_type=jnp.float32
    )


def contract_first(left, right):
    return lax.dot_general(
        left, right, (((0,), (0,)), ((), ())), preferred_element_type=jnp.float32
    )


def expert_kernel(
    capacity,
    normed,
    grads,
    routes,
    router_rows,
    w_gate,
    w_up,
    w_down,
    shared_in,
    shared_out,
    out_part,
    d_part,
    ex_rows,
    ex_grads,
    act_out,
    d_gate_out,
    d_up_out,
    shared_in_grad,
    shared_out_grad,
    in_total,
    out_total,
):
    position = lax.axis_index("expert")
    experts = lax.axis_size("expert")
    group, rows, width = normed.shape
    tokens, slots = group * rows, group * capacity
    bf16 = jnp.bfloat16
    x = normed[...].reshape(tokens, width)
    g = grads[...].reshape(tokens, width)

    row = lax.broadcasted_iota(jnp.int32, (tokens, tokens), 0)
    column = lax.broadcasted_iota(jnp.int32, (tokens, tokens), 1)
    before = jnp.logical_and(column < row, lax.div(row, rows) == lax.div(column, rows))
    named = routes[...].reshape(tokens, -1) == position.astype(jnp.float32).astype(bf16)
    hit = jnp.sum(jnp.where(named, 1.0, 0.0), axis=1, keepdims=True)
    tally = matrix_product(
        jnp.where(before, 1.0, 0.0).astype(bf16),
        jnp.broadcast_to(hit, (tokens, 128)).astype(bf16),
    )
    place = jnp.where(hit > 0.5, tally[:, :1], -1.0)
    token = lax.broadcasted_iota(jnp.int32, (tokens, slots), 0)
    slot = lax.broadcasted_iota(jnp.int32, (tokens, slots), 1)
    same = lax.div(slot, capacity) == lax.div(token, rows)
    wanted = lax.rem(slot, capacity).astype(jnp.float32)
    chosen = jnp.where(jnp.logical_and(same, wanted == place), 1.0, 0.0)
    pick = chosen.T.astype(bf16)
    put = chosen.astype(bf16)

    r = matrix_product(pick, x).astype(bf16)
    gr = matrix_product(pick, g).astype(bf16)
    ex_rows[...] = r
    ex_grads[...] = gr
    lane = lax.broadcasted_iota(jnp.int32, (slots, router_rows.shape[0]), 1)
    logits = jnp.where(lane < experts, contract_last(r, router_rows[...]), -1e30)
    exps = jnp.exp(logits - jnp.max(logits, axis=1, keepdims=True))
    gate = jnp.sum(jnp.where(lane == position, exps, 0.0), axis=1, keepdims=True) / jnp.sum(
        exps, axis=1, keepdims=True
    )

    pre_gate = contract_last(r, w_gate[...])
    pre_up = contract_last(r, w_up[...])
    act_gate, slope = silu_parts(pre_gate)
    act = act_gate * pre_up
    back = contract_last(gr, w_down[...])
    d_gate_slot = jnp.sum(act * back, axis=1, keepdims=True)
    scaled = (gate * act).astype(bf16)
    d_act = gate * back
    d_pre_gate = (d_act * pre_up * slope).astype(bf16)
    d_pre_up = (d_act * act_gate).astype(bf16)
    act_out[...] = scaled
    d_gate_out[...] = d_pre_gate
    d_up_out[...] = d_pre_up
    ex_out = matrix_product(scaled, w_down[...]).astype(bf16)
    d_ex = matrix_product(d_pre_gate, w_gate[...]) + matrix_product(d_pre_up, w_up[...])
    d_ex = d_ex.astype(bf16)

    units = shared_out.shape[0]
    mix = matrix_product(x, shared_in[...])
    sh_gate, sh_up = mix[:, :units], mix[:, units:]
    sh_silu, sh_slope = silu_parts(sh_gate)
    sh_act = (sh_silu * sh_up).astype(bf16)
    d_sh_act = contract_last(g, shared_out[...])
    d_mix = jnp.concatenate([d_sh_act * sh_up * sh_slope, d_sh_act * sh_silu], axis=1)
    d_mix = d_mix.astype(bf16)

    out = matrix_product(put, ex_out) + matrix_product(sh_act, shared_out[...])
    out_part[...] = out.astype(bf16).reshape(group, rows, width)
    d_in = matrix_product(put, d_ex) + contract_last(d_mix, shared_in[...])
    d_part[:, :, :width] = d_in.astype(bf16).reshape(group, rows, width)
    lane = lax.broadcasted_iota(jnp.int32, (slots, d_part.shape[2] - width), 1)
    d_gates = jnp.where(lane == position, d_gate_slot, 0.0).astype(bf16)
    d_part[:, :, width:] = matrix_product(put, d_gates).astype(bf16).reshape(group, rows, -1)

    step = pl.program_id(0)

    @pl.when(step == 0)
    def _():
        in_total[...] = jnp.zeros_like(in_total)
        out_total[...] = jnp.zeros_like(out_total)

    in_total[...] += contract_first(d_mix, x)
    out_total[...] += contract_first(sh_act, g)

    @pl.when(step == pl.num_programs(0) - 1)
    def _():
        shared_in_grad[...] = in_total[...].T.astype(bf16)
        shared_out_grad[...] = out_total[...]


def expert_phase(
    all_normed, all_grads, router_rows, w_gate, w_up, w_down, shared_in, shared_out, capacity
):
    blocks, rows, width = all_normed.shape
    group = 4
    slots = group * capacity
    hidden = w_gate.shape[0]
    units = shared_out.shape[0]
    side = all_grads.shape[2] - width
    bf16 = jnp.bfloat16

    def by_group(shape):
        zeros = (0,) * (len(shape) - 1)
        return pl.BlockSpec(shape, lambda i: (i,) + zeros)

    def fixed(shape):
        return pl.BlockSpec(
            shape, lambda i: (0,) * len(shape), pipeline_mode=pl.Buffered(buffer_count=1)
        )

    return pl.pallas_call(
        functools.partial(expert_kernel, capacity),
        grid=(blocks // group,),
        out_shape=[
            jax.ShapeDtypeStruct((blocks, rows, width), bf16),
            jax.ShapeDtypeStruct((blocks, rows, width + side), bf16),
            jax.ShapeDtypeStruct((blocks * capacity, width), bf16),
            jax.ShapeDtypeStruct((blocks * capacity, width), bf16),
            jax.ShapeDtypeStruct((blocks * capacity, hidden), bf16),
            jax.ShapeDtypeStruct((blocks * capacity, hidden), bf16),
            jax.ShapeDtypeStruct((blocks * capacity, hidden), bf16),
            jax.ShapeDtypeStruct((width, 2 * units), bf16),
            jax.ShapeDtypeStruct((units, width), jnp.float32),
        ],
        in_specs=[
            by_group((group, rows, width)),
            by_group((group, rows, width)),
            pl.BlockSpec((group, rows, side), lambda i: (i, 0, width // side)),
            fixed(router_rows.shape),
            fixed(w_gate.shape),
            fixed(w_up.shape),
            fixed(w_down.shape),
            fixed(shared_in.shape),
            fixed(shared_out.shape),
        ],
        out_specs=[
            by_group((group, rows, width)),
            by_group((group, rows, width + side)),
            by_group((slots, width)),
            by_group((slots, width)),
            by_group((slots, hidden)),
            by_group((slots, hidden)),
            by_group((slots, hidden)),
            fixed((width, 2 * units)),
            fixed((units, width)),
        ],
        scratch_shapes=[
            pltpu.VMEM((2 * units, width), jnp.float32),
            pltpu.VMEM((units, width), jnp.float32),
        ],
        compiler_params=pltpu.CompilerParams(vmem_limit_bytes=VMEM_LIMIT),
        cost_estimate=pl.CostEstimate(
            flops=2 * blocks * capacity * width * hidden * 6,
            bytes_accessed=10 * blocks * rows * width * 2,
            transcendentals=blocks * capacity * hidden,
        ),
    )(all_normed, all_grads, all_grads, router_rows, w_gate, w_up, w_down, shared_in, shared_out)


def exchange_kernel(x, out, local_sem, send_sems, recv_sems):
    me, y = lax.axis_index("expert"), lax.axis_index("fsdp")
    count = x.shape[0]
    barrier = pltpu.get_barrier_semaphore()
    peers = [lax.rem(me + step, count) for step in range(1, count)]
    for peer in peers:
        pl.semaphore_signal(barrier, inc=1, device_id=(peer, y), device_id_type=MESH)
    own = pltpu.make_async_copy(x.at[me], out.at[me], local_sem)
    own.start()
    pl.semaphore_wait(barrier, count - 1)
    copies = []
    for at, peer in enumerate(peers):
        copy = pltpu.make_async_remote_copy(
            src_ref=x.at[peer],
            dst_ref=out.at[me],
            send_sem=send_sems.at[at],
            recv_sem=recv_sems.at[at],
            device_id=(peer, y),
            device_id_type=MESH,
        )
        copy.start()
        copies.append(copy)
    for copy in copies:
        copy.wait()
    own.wait()


def exchange(x, collective_id):
    count = x.shape[0]
    return pl.pallas_call(
        exchange_kernel,
        out_shape=jax.ShapeDtypeStruct(x.shape, x.dtype),
        in_specs=[pl.BlockSpec(memory_space=pl.ANY)],
        out_specs=pl.BlockSpec(memory_space=pl.ANY),
        scratch_shapes=[
            pltpu.SemaphoreType.DMA,
            pltpu.SemaphoreType.DMA((count - 1,)),
            pltpu.SemaphoreType.DMA((count - 1,)),
        ],
        compiler_params=pltpu.CompilerParams(collective_id=collective_id, has_side_effects=True),
        cost_estimate=pl.CostEstimate(
            flops=0, bytes_accessed=20 * x.size * x.dtype.itemsize, transcendentals=0
        ),
    )(x)


def swap_halves(value):
    half = value.shape[1] // 2
    return jnp.concatenate([value[:, half:], value[:, :half]], axis=1)


def greet_plane(place):
    me = lax.axis_index("expert")
    count = LINE * SQUARE * CORES
    barrier = pltpu.get_barrier_semaphore()
    for step in range(1, count):
        peer = (lax.rem(me + step, count), place.y)
        pl.semaphore_signal(barrier, inc=1, device_id=peer, device_id_type=MESH)
    pl.semaphore_signal(barrier, inc=1, device_id=place.device(dy=1), device_id_type=MESH)
    pl.semaphore_wait(barrier, count)


def sums_kernel(pairs, moved, small, large, *refs):
    ins = refs[:pairs]
    moved_out, small_out, large_out = refs[pairs : pairs + 3]
    outs = refs[pairs + 3 : 2 * pairs + 3]
    rest = refs[2 * pairs + 3 :]
    local_sem, exchange_sends, exchange_recvs = rest[:3]
    first, second = rest[3:12], rest[12:21]
    place = Place()
    me = lax.axis_index("expert")
    count = moved.shape[0]
    greet_plane(place)
    own = pltpu.make_async_copy(moved.at[me], moved_out.at[me], local_sem)
    own.start()
    copies = []
    for at in range(count - 1):
        copy = pltpu.make_async_remote_copy(
            src_ref=moved.at[lax.rem(me + at + 1, count)],
            dst_ref=moved_out.at[me],
            send_sem=exchange_sends.at[at],
            recv_sem=exchange_recvs.at[at],
            device_id=(lax.rem(me + at + 1, count), place.y),
            device_id_type=MESH,
        )
        copy.start()
        copies.append(copy)
    senders = [Sender(place, first[6]), Sender(place, second[6])]
    send_pairs(senders[0], ins, outs, first[8])
    ticks = [
        scatter_ticks(place, senders[0], False, small, small_out, first[:6] + (first[7],)),
        scatter_ticks(place, senders[1], True, large, large_out, second[:6] + (second[7],)),
    ]
    for number in range(max(len(steps) for steps in ticks)):
        for steps in ticks:
            if number < len(steps):
                steps[number]()
    take_pairs(senders[0], outs, first[8])
    for sender in senders:
        sender.finish()
    for copy in copies:
        copy.wait()
    own.wait()


def exchange_and_sums(moved, small, large, swapped, collective_id):
    count, pairs = moved.shape[0], len(swapped)
    hbm = pl.BlockSpec(memory_space=pl.ANY)
    vmem = pl.BlockSpec(memory_space=pltpu.VMEM)
    return pl.pallas_call(
        functools.partial(sums_kernel, pairs),
        out_shape=[
            jax.ShapeDtypeStruct(moved.shape, moved.dtype),
            jax.ShapeDtypeStruct(small.shape[1:], jnp.float32),
            jax.ShapeDtypeStruct(large.shape[1:], jnp.float32),
        ]
        + [jax.ShapeDtypeStruct(x.shape, x.dtype) for x in swapped],
        in_specs=[hbm] * (3 + pairs),
        out_specs=[hbm, vmem, vmem] + [hbm] * pairs,
        scratch_shapes=[
            pltpu.SemaphoreType.DMA,
            pltpu.SemaphoreType.DMA((count - 1,)),
            pltpu.SemaphoreType.DMA((count - 1,)),
        ]
        + scatter_scratch(False, *small.shape[1:], small.dtype, pairs)
        + scatter_scratch(True, *large.shape[1:], large.dtype, 0),
        compiler_params=pltpu.CompilerParams(
            collective_id=collective_id, has_side_effects=True, vmem_limit_bytes=VMEM_LIMIT
        ),
        cost_estimate=pl.CostEstimate(
            flops=0, bytes_accessed=12 * large.size * 2, transcendentals=0
        ),
    )(moved, small, large, *swapped)


def attend_kernel(
    rows,
    g_attn,
    w_front,
    g_lat,
    expand_head,
    cosines,
    sines,
    normed_out,
    latent_out,
    query_out,
    key_out,
    value_out,
    head_out,
    sum_out,
    log_out,
    keys,
    values,
):
    bf16 = jnp.bfloat16
    size = rows.shape[0]
    scale = (PLAIN_UNITS + ROTARY_UNITS) ** (-0.5)
    step = pl.program_id(0)
    normed, _ = norm_forward(rows[...].astype(jnp.float32), g_attn[...])
    normed = normed.astype(bf16)
    normed_out[...] = normed
    front = contract_last(normed, w_front[...])
    latent, _ = norm_forward(front[:, :LATENT_WIDTH], g_lat[...])
    latent = latent.astype(bf16)
    latent_out[...] = latent
    width = LATENT_WIDTH + ROTARY_UNITS

    def rotated(value):
        return value * cosines[...] + swap_halves(value) * sines[...]

    pairs = matrix_product(latent, expand_head[...])
    key = jnp.concatenate([pairs[:, :PLAIN_UNITS], rotated(front[:, LATENT_WIDTH:width])], axis=1)
    query = jnp.concatenate(
        [front[:, width : width + PLAIN_UNITS], rotated(front[:, width + PLAIN_UNITS :])], axis=1
    ).astype(bf16)
    key = key.astype(bf16)
    value = pairs[:, PLAIN_UNITS:].astype(bf16)
    query_out[...] = query
    key_out[...] = key
    value_out[...] = value
    here = pl.ds(pl.multiple_of(step * size, size), size)
    keys[here, :] = key
    values[here, :] = value
    row = lax.broadcasted_iota(jnp.int32, (size, size), 0)
    column = lax.broadcasted_iota(jnp.int32, (size, size), 1)
    near = jnp.where(column <= row, contract_last(query, key) * scale, -1e30)

    def over(past):
        top = jnp.max(near, axis=1, keepdims=True)
        if past:
            far = contract_last(query, keys[:past, :]) * scale
            top = jnp.maximum(top, jnp.max(far, axis=1, keepdims=True))
        exps = jnp.exp(near - top)
        total = jnp.sum(exps, axis=1, keepdims=True)
        mixed = matrix_product(exps.astype(bf16), value)
        if past:
            exps = jnp.exp(far - top)
            total = total + jnp.sum(exps, axis=1, keepdims=True)
            mixed = mixed + matrix_product(exps.astype(bf16), values[:past, :])
        mixed = mixed / total
        sum_out[...] = mixed
        head_out[...] = mixed.astype(bf16)
        wide = jnp.broadcast_to(top + jnp.log(total), (size, 128))
        log_out[0] = wide.T[:1, :]

    for at in range(keys.shape[0] // size):
        pl.when(step == at)(functools.partial(over, at * size))


def attend(rows, g_attn, w_front, g_lat, expand_head, cosines, sines):
    seq_len, width = rows.shape
    size = 256
    steps = seq_len // size
    units = PLAIN_UNITS + ROTARY_UNITS
    bf16 = jnp.bfloat16

    def by_step(columns):
        return pl.BlockSpec((size, columns), lambda i: (i, 0))

    def fixed(x):
        return pl.BlockSpec(
            x.shape, lambda i: (0, 0), pipeline_mode=pl.Buffered(buffer_count=1)
        )

    return pl.pallas_call(
        attend_kernel,
        grid=(steps,),
        out_shape=[
            jax.ShapeDtypeStruct((seq_len, width), bf16),
            jax.ShapeDtypeStruct((seq_len, LATENT_WIDTH), bf16),
            jax.ShapeDtypeStruct((seq_len, units), bf16),
            jax.ShapeDtypeStruct((seq_len, units), bf16),
            jax.ShapeDtypeStruct((seq_len, VALUE_UNITS), bf16),
            jax.ShapeDtypeStruct((seq_len, VALUE_UNITS), bf16),
            jax.ShapeDtypeStruct((seq_len, VALUE_UNITS), jnp.float32),
            jax.ShapeDtypeStruct((steps, 1, size), jnp.float32),
        ],
        in_specs=[by_step(width)]
        + [fixed(x) for x in (g_attn, w_front, g_lat, expand_head)]
        + [by_step(ROTARY_UNITS)] * 2,
        out_specs=[
            by_step(width),
            by_step(LATENT_WIDTH),
            by_step(units),
            by_step(units),
            by_step(VALUE_UNITS),
            by_step(VALUE_UNITS),
            by_step(VALUE_UNITS),
            pl.BlockSpec((1, 1, size), lambda i: (i, 0, 0)),
        ],
        scratch_shapes=[
            pltpu.VMEM((seq_len, units), bf16),
            pltpu.VMEM((seq_len, VALUE_UNITS), bf16),
        ],
        compiler_params=pltpu.CompilerParams(vmem_limit_bytes=VMEM_LIMIT),
        cost_estimate=pl.CostEstimate(
            flops=2 * seq_len * (width * 768 + seq_len * units),
            bytes_accessed=3 * rows.size * 2,
            transcendentals=seq_len * seq_len // 2,
        ),
    )(rows, g_attn, w_front, g_lat, expand_head, cosines, sines)


def attend_back_kernel(
    query,
    key,
    value,
    d_head,
    head_sum,
    logs,
    expand_head,
    cosines,
    sines,
    d_query_out,
    d_pairs_out,
    d_keys_out,
    d_key,
    d_value,
    key_turned,
):
    bf16 = jnp.bfloat16
    size = query.shape[0]
    seq_len = key.shape[0]
    scale = (PLAIN_UNITS + ROTARY_UNITS) ** (-0.5)
    step = pl.program_id(0)

    @pl.when(step == 0)
    def _():
        d_key[...] = jnp.zeros_like(d_key)
        d_value[...] = jnp.zeros_like(d_value)
        for at in range(0, seq_len, size):
            part = key[at : at + size, :].astype(jnp.float32)
            key_turned[:, at : at + size] = part.T.astype(bf16)

    q, d_out = query[...], d_head[...]
    product = d_out.astype(jnp.float32) * head_sum[...]
    delta = jnp.sum(product.T, axis=0, keepdims=True)
    log_row = logs[0]
    row = lax.broadcasted_iota(jnp.int32, (size, size), 0)
    column = lax.broadcasted_iota(jnp.int32, (size, size), 1)

    def grads_of(at, mask):
        there = slice(at, at + size)
        scores = contract_last(key[there, :], q) * scale
        if mask:
            scores = jnp.where(row <= column, scores, -1e30)
        probs = jnp.exp(scores - log_row)
        d_probs = contract_last(value[there, :], d_out)
        d_scores = (probs * (d_probs - delta) * scale).astype(bf16)
        d_key[there, :] += matrix_product(d_scores, q)
        d_value[there, :] += matrix_product(probs.astype(bf16), d_out)
        return matrix_product(key_turned[:, there], d_scores)

    def over(past):
        total = grads_of(past, True)
        for at in range(0, past, size):
            total = total + grads_of(at, False)
        d_query = total.T
        d_rope = d_query[:, PLAIN_UNITS:]
        d_rope = d_rope * cosines[...] - swap_halves(d_rope) * sines[...]
        d_query_out[...] = jnp.concatenate([d_query[:, :PLAIN_UNITS], d_rope], axis=1).astype(bf16)

    for at in range(seq_len // size):
        pl.when(step == at)(functools.partial(over, at * size))

    @pl.when(step == seq_len // size - 1)
    def _():
        for at in range(0, seq_len, size):
            there = slice(at, at + size)
            d_pairs = jnp.concatenate(
                [d_key[there, :PLAIN_UNITS], d_value[there, :]], axis=1
            ).astype(bf16)
            d_pairs_out[there, :] = d_pairs
            d_keys_out[there, :LATENT_WIDTH] = contract_last(d_pairs, expand_head[...]).astype(bf16)
            tail = jnp.concatenate(
                [d_key[there, PLAIN_UNITS:], jnp.zeros((size, ROTARY_UNITS), jnp.float32)], axis=1
            )
            d_keys_out[there, LATENT_WIDTH:] = tail.astype(bf16)


def attend_back(query, key, value, d_head, head_sum, logs, expand_head, cosines, sines):
    seq_len, units = query.shape
    steps, _, size = logs.shape
    bf16 = jnp.bfloat16
    keys_width = LATENT_WIDTH + 2 * ROTARY_UNITS

    def by_step(columns):
        return pl.BlockSpec((size, columns), lambda i: (i, 0))

    def fixed(shape):
        return pl.BlockSpec(shape, lambda i: (0, 0), pipeline_mode=pl.Buffered(buffer_count=1))

    return pl.pallas_call(
        attend_back_kernel,
        grid=(steps,),
        out_shape=[
            jax.ShapeDtypeStruct((seq_len, units), bf16),
            jax.ShapeDtypeStruct((seq_len, PLAIN_UNITS + VALUE_UNITS), bf16),
            jax.ShapeDtypeStruct((seq_len, keys_width), bf16),
        ],
        in_specs=[
            by_step(units),
            fixed(key.shape),
            fixed(value.shape),
            by_step(VALUE_UNITS),
            by_step(VALUE_UNITS),
            pl.BlockSpec((1, 1, size), lambda i: (i, 0, 0)),
            fixed(expand_head.shape),
            by_step(ROTARY_UNITS),
            by_step(ROTARY_UNITS),
        ],
        out_specs=[
            by_step(units),
            fixed((seq_len, PLAIN_UNITS + VALUE_UNITS)),
            fixed((seq_len, keys_width)),
        ],
        scratch_shapes=[
            pltpu.VMEM((seq_len, units), jnp.float32),
            pltpu.VMEM((seq_len, VALUE_UNITS), jnp.float32),
            pltpu.VMEM((units, seq_len), bf16),
        ],
        compiler_params=pltpu.CompilerParams(vmem_limit_bytes=VMEM_LIMIT),
        cost_estimate=pl.CostEstimate(
            flops=5 * seq_len * seq_len * units,
            bytes_accessed=8 * seq_len * units * 2,
            transcendentals=seq_len * seq_len // 2,
        ),
    )(query, key, value, d_head, head_sum, logs, expand_head, cosines, sines)


def finish_kernel(query, expand, out_rows, query_out, expand_out, out_out):
    heads, units, width = query.shape
    query_out[...] = query[...].reshape(heads * units, width).astype(jnp.float32).T
    for at in range(heads):
        columns = expand.shape[2]
        expand_out[:, at * columns : (at + 1) * columns] = expand[at].astype(jnp.float32)
    out_out[...] = out_rows[...].reshape(out_out.shape).astype(jnp.float32)


def finish(query, expand, out_rows):
    heads, units, width = query.shape
    _, latents, columns = expand.shape
    _, rows, model = out_rows.shape
    return pl.pallas_call(
        finish_kernel,
        grid=(heads // 2,),
        out_shape=[
            jax.ShapeDtypeStruct((width, heads * units), jnp.float32),
            jax.ShapeDtypeStruct((latents, heads * columns), jnp.float32),
            jax.ShapeDtypeStruct((heads * rows, model), jnp.float32),
        ],
        in_specs=[
            pl.BlockSpec((2, units, width), lambda i: (i, 0, 0)),
            pl.BlockSpec((2, latents, columns), lambda i: (i, 0, 0)),
            pl.BlockSpec((2, rows, model), lambda i: (i, 0, 0)),
        ],
        out_specs=[
            pl.BlockSpec((width, 2 * units), lambda i: (0, i)),
            pl.BlockSpec((latents, 2 * columns), lambda i: (0, i)),
            pl.BlockSpec((2 * rows, model), lambda i: (i, 0)),
        ],
        compiler_params=pltpu.CompilerParams(vmem_limit_bytes=VMEM_LIMIT),
        cost_estimate=pl.CostEstimate(
            flops=0, bytes_accessed=6 * heads * units * width, transcendentals=0
        ),
    )(query, expand, out_rows)


def token_gather(rows):
    return lax.all_gather(rows, ("fsdp", "expert"), axis=0, tiled=True)


def split_body(
    tokens,
    routes,
    cotangent,
    attn_gain,
    w_query,
    latent_weight,
    latent_norm_gain,
    expand_weight,
    w_out,
    ffn_gain,
    w_router,
    shared_gate,
    shared_up,
    shared_down,
    expert_gate,
    expert_up,
    expert_down,
):
    rows = tokens.shape[1]
    experts = lax.axis_size("expert")
    shards = lax.axis_size("fsdp")
    position = lax.axis_index("expert")
    blocks = experts * shards
    seq_len = rows * experts
    capacity = shards * ((rows * TOPK * 4 + experts * 3 * shards - 1) // (experts * 3 * shards))
    head_units = PLAIN_UNITS + ROTARY_UNITS
    pair_units = PLAIN_UNITS + VALUE_UNITS
    feature_width = LATENT_WIDTH + ROTARY_UNITS
    scale = head_units ** (-0.5)

    shard = lax.axis_index("fsdp")
    first = shard == 0

    query_cols = lax.dynamic_slice_in_dim(w_query, position * head_units, head_units, 1)
    expand_cols = lax.dynamic_slice_in_dim(expand_weight, position * pair_units, pair_units, 1)
    owners = experts // shards
    lat_row = jnp.pad(latent_norm_gain, (0, w_query.shape[0] - latent_norm_gain.shape[0]))
    packed = jnp.concatenate(
        [query_cols.T, w_router.T, attn_gain[None], ffn_gain[None], lat_row[None]],
        axis=0,
    )
    packed = jnp.pad(packed, ((0, -packed.shape[0] % 32), (0, 0)))
    seq_rows, other_packed, other_expand, other_latent = gather_rows(
        [tokens[0]], False, 0, swapped=[packed, expand_cols], halved=[latent_weight.T]
    )

    def whole(own, other, axis):
        return jnp.concatenate(
            [jnp.where(first, own, other), jnp.where(first, other, own)], axis=axis
        )

    lat_half = latent_norm_gain.shape[0]
    at = head_units
    packed_rows = whole(packed, other_packed, 1)
    expand_head = whole(expand_cols, other_expand, 0)
    w_latent = whole(latent_weight.T, other_latent, 1)
    w_front = jnp.concatenate([w_latent, packed_rows[:at]], axis=0)
    router_rows = packed_rows[at:]
    wrout = packed_rows[at : at + experts]
    g_attn = packed_rows[at + experts].astype(jnp.float32)
    g_ffn = packed_rows[at + experts + 1].astype(jnp.float32)
    lat_row = packed_rows[at + experts + 2]
    g_lat = jnp.concatenate(
        [lat_row[:lat_half], lat_row[w_query.shape[0] : w_query.shape[0] + lat_half]]
    ).astype(jnp.float32)
    units = shared_down.shape[0]

    core = lax.rem(position, CORES)

    def by_cores(weight):
        size = weight.shape[0] // CORES
        own = lax.dynamic_slice_in_dim(weight, core * size, size, 0)
        own = lax.all_gather(own, "fsdp", axis=0, tiled=True)
        swap = [(index, index ^ 1) for index in range(experts)]
        return own, lax.ppermute(own, "expert", swap)

    def core_columns(value, which):
        size = value.shape[1] // (CORES * shards)
        parts = [
            lax.dynamic_slice_in_dim(value, (at * CORES + which) * size, size, 1)
            for at in range(shards)
        ]
        return jnp.concatenate(parts, axis=1)

    def in_order(own, other):
        lower, upper = jnp.where(core == 0, own, other), jnp.where(core == 0, other, own)
        size = own.shape[1] // shards
        parts = []
        for at in range(shards):
            parts += [lower[:, at * size : (at + 1) * size], upper[:, at * size : (at + 1) * size]]
        return jnp.concatenate(parts, axis=1)

    out_own, out_other = by_cores(w_out)
    grad_rows = cotangent[0]
    grad_out = grad_rows.astype(jnp.float32)
    own_routes = jnp.pad(routes[0], ((0, 0), (0, 128 - TOPK)), constant_values=-1)
    grad_rows = jnp.concatenate([grad_rows, own_routes.astype(jnp.bfloat16)], axis=1)
    seq_rows, grad_rows, shared_gate, shared_up = lax.optimization_barrier(
        (seq_rows, grad_rows, shared_gate, shared_up)
    )
    def to_columns(weight):
        parts = weight.reshape(weight.shape[0], blocks, units).transpose(1, 0, 2)
        return lax.all_to_all(
            parts, ("expert", "fsdp"), split_axis=0, concat_axis=0, tiled=True
        ).reshape(-1, units)

    sh_cols = to_columns(jnp.concatenate([shared_gate, shared_up], axis=0)).reshape(
        blocks, 2, shared_gate.shape[0], units
    )
    lanes = -(-units // 128) * 128
    sh_cols = jnp.pad(sh_cols, ((0, 0), (0, 0), (0, 0), (0, lanes - units)))
    shared_in = sh_cols.transpose(0, 2, 1, 3).reshape(MODEL_WIDTH, 2 * lanes)
    shared_out = jnp.pad(shared_down, ((0, lanes - units), (0, 0)))
    all_grads = token_gather(grad_rows)

    x_in = tokens[0].astype(jnp.float32)
    normed, inv_attn = norm_forward(x_in, g_attn)
    normed_in = normed.astype(jnp.bfloat16)
    half_units = ROTARY_UNITS // 2
    freqs = 10000.0 ** (-np.arange(half_units) * (2.0 / ROTARY_UNITS))
    angles = np.arange(seq_len)[:, None] * freqs[None, :]
    cosine_table = jnp.asarray(np.cos(angles), jnp.float32)
    sine_table = jnp.asarray(np.sin(angles), jnp.float32)
    cosines = jnp.asarray(np.concatenate([np.cos(angles)] * 2, axis=1), jnp.float32)
    sines = jnp.asarray(np.concatenate([-np.sin(angles), np.sin(angles)], axis=1), jnp.float32)
    (
        seq_normed,
        latent_rows,
        query,
        key,
        value,
        head_rows,
        head_sum,
        logs,
    ) = attend(
        seq_rows.reshape(seq_len, MODEL_WIDTH),
        g_attn[None],
        w_front,
        g_lat[None],
        expand_head,
        cosines,
        sines,
    )
    head_rows, shared_in = lax.optimization_barrier((head_rows, shared_in))
    heads = exchange(head_rows.reshape(experts, rows, VALUE_UNITS), 1)
    heads = heads.transpose(1, 0, 2).reshape(rows, experts * VALUE_UNITS)
    hidden = x_in + matrix_product(core_columns(heads, core), out_own)
    hidden = hidden + matrix_product(core_columns(heads, 1 - core), out_other)
    normed2, inv_ffn = norm_forward(hidden, g_ffn)
    normed_ffn = normed2.astype(jnp.bfloat16)
    router = jax.nn.softmax(outer_product(normed_ffn, wrout), axis=-1)

    (all_normed,) = gather_rows([normed_ffn], True, 2)
    w_query, all_normed = lax.optimization_barrier((w_query, all_normed))
    query_own, query_other = by_cores(w_query)
    (
        out_part,
        d_part,
        ex_rows,
        ex_grads,
        scaled_act,
        d_pre_gate,
        d_pre_up,
        g_shared_in,
        g_shared_out,
    ) = expert_phase(
        all_normed,
        all_grads.reshape(blocks, rows, -1),
        router_rows,
        expert_gate[0].T,
        expert_up[0].T,
        expert_down[0],
        shared_in,
        shared_out,
        capacity,
    )
    g_down = inner(scaled_act, ex_grads)
    g_gate = inner(d_pre_gate, ex_rows).T
    g_up = inner(d_pre_up, ex_rows).T
    (d_back,) = scatter_rows(d_part, True, 3)
    out_part, d_back = lax.optimization_barrier((out_part, d_back))
    out_sum = lax.psum_scatter(
        out_part.reshape(blocks * rows, MODEL_WIDTH),
        ("fsdp", "expert"),
        scatter_dimension=0,
        tiled=True,
    )
    d_normed_ffn = d_back[:, :MODEL_WIDTH]
    d_router = d_back[:, MODEL_WIDTH : MODEL_WIDTH + experts]

    d_logits = (router * (d_router - jnp.sum(router * d_router, axis=1, keepdims=True))).astype(
        jnp.bfloat16
    )
    g_router = inner(d_logits, normed_ffn)
    d_normed_ffn = d_normed_ffn + matrix_product(d_logits, wrout)
    d_hidden_norm, g_ffn_grad = norm_backward(hidden, inv_ffn, g_ffn, d_normed_ffn)
    d_hidden = grad_out + d_hidden_norm
    d_attn = d_hidden.astype(jnp.bfloat16)

    d_heads = in_order(outer_product(d_attn, out_own), outer_product(d_attn, out_other))
    d_heads = d_heads.astype(jnp.bfloat16)
    d_heads = d_heads.reshape(rows, experts, VALUE_UNITS).transpose(1, 0, 2)
    d_head = exchange(d_heads, 4).reshape(seq_len, VALUE_UNITS)
    out_grad_part = inner(heads, d_attn).astype(jnp.bfloat16)
    d_query_full, d_pairs, d_keys = attend_back(
        query, key, value, d_head, head_sum, logs, expand_head, cosines, sines
    )
    g_expand_head = inner(latent_rows, d_pairs)
    g_query_head = inner(d_query_full, seq_normed).astype(jnp.bfloat16)
    g_expand_head = g_expand_head.astype(jnp.bfloat16)

    def half_of(whole, which, axis):
        size = whole.shape[axis] // shards
        return lax.dynamic_slice_in_dim(whole, which * size, size, axis)

    own_d_query, d_sums, own_out, other_query, other_expand = exchange_and_sums(
        d_query_full.reshape(experts, rows, head_units),
        d_keys.reshape(experts, rows, -1),
        out_grad_part.reshape(blocks, -1, MODEL_WIDTH),
        [half_of(g_query_head, 1 - shard, 1), half_of(g_expand_head, 1 - shard, 0)],
        5,
    )
    own_d_query = own_d_query.transpose(1, 0, 2).reshape(rows, experts * head_units)
    key_gradient = d_sums[:, :feature_width]
    d_normed_in = in_order(
        outer_product(own_d_query, query_own), outer_product(own_d_query, query_other)
    )

    def summed(own, other):
        return (own.astype(jnp.float32) + other.astype(jnp.float32)).astype(jnp.bfloat16)

    own_query = summed(half_of(g_query_head, shard, 1), other_query)
    own_expand = summed(half_of(g_expand_head, shard, 0), other_expand)
    own_out = own_out.astype(jnp.bfloat16)
    own_latent = outer_product(normed_in, w_latent[:LATENT_WIDTH])
    own_cosine = lax.dynamic_slice_in_dim(cosine_table, position * rows, rows, 0)
    own_sine = lax.dynamic_slice_in_dim(sine_table, position * rows, rows, 0)
    inv_lat = lax.rsqrt(jnp.mean(own_latent * own_latent, axis=-1, keepdims=True) + EPS)
    d_compact, g_lat_grad = norm_backward(
        own_latent, inv_lat, g_lat, key_gradient[:, :LATENT_WIDTH]
    )
    d_rope = reverse_rotary(key_gradient[:, LATENT_WIDTH:], own_cosine, own_sine)
    d_latent_full = jnp.concatenate([d_compact, d_rope], axis=-1).astype(jnp.bfloat16)
    g_latent = inner(d_latent_full, normed_in)
    d_normed_in = d_normed_in + matrix_product(d_latent_full, w_latent)
    d_norm_in, g_attn_grad = norm_backward(x_in, inv_attn, g_attn, d_normed_in)
    d_tokens = (d_hidden + d_norm_in).astype(jnp.bfloat16)

    half = MODEL_WIDTH // blocks
    cols = lax.all_to_all(
        g_shared_in.reshape(blocks, half, 2 * lanes),
        ("expert", "fsdp"),
        split_axis=0,
        concat_axis=0,
        tiled=True,
    )
    cols = cols.transpose(1, 0, 2).astype(jnp.float32)
    r_sgate = cols[:, :, :units].reshape(half, blocks * units)
    r_sup = cols[:, :, lanes : lanes + units].reshape(half, blocks * units)
    g_sdown = g_shared_out[:units]
    model_half = MODEL_WIDTH // shards
    small_rows = jnp.concatenate([g_latent, g_router, g_attn_grad[None], g_ffn_grad[None]], axis=0)
    used = small_rows.shape[0]
    share = 2 * 32 * (-(-(used + 1) // (2 * 32 * experts)))

    def rows_for(which):
        here = small_rows[:, which * model_half : (which + 1) * model_half]
        lat = jnp.pad(
            g_lat_grad[which * lat_half : (which + 1) * lat_half], (0, model_half - lat_half)
        )
        full = jnp.concatenate([here, lat[None]], axis=0).astype(jnp.bfloat16)
        full = jnp.pad(full, ((0, experts * share - used - 1), (0, 0)))
        return full.reshape(experts, share, model_half)

    small_part = jnp.concatenate([rows_for(which) for which in range(shards)], axis=0)
    r_query, r_expand, r_out, small_sum = gather_and_scatter(
        [own_query, own_expand, own_out], small_part, 6
    )
    hidden, small_sum = lax.optimization_barrier((hidden, small_sum))
    output = hidden + out_sum.astype(jnp.float32)
    (small_all,) = gather_rows([small_sum.astype(jnp.bfloat16)], False, 7)
    r_query, r_expand, r_out = finish(r_query, r_expand, r_out)
    small_all = small_all.reshape(experts * share, model_half).astype(jnp.float32)
    return (
        output.astype(jnp.bfloat16)[None],
        d_tokens[None],
        small_all[feature_width + experts],
        r_query,
        small_all[:feature_width].T,
        small_all[feature_width + experts + 2, :lat_half],
        r_expand,
        r_out,
        small_all[feature_width + experts + 1],
        small_all[feature_width : feature_width + experts].T,
        r_sgate,
        r_sup,
        g_sdown,
        g_gate[None],
        g_up[None],
        g_down[None],
    )


def solution(mesh):
    shape = (mesh.shape["expert"], mesh.shape["fsdp"])
    split = shape == (LINE * SQUARE * CORES, SQUARE) and shape[0] == HEAD_COUNT
    return jax.shard_map(
        split_body if split else body,
        mesh=mesh,
        in_specs=(
            P("fsdp", "expert", None),
            P("fsdp", "expert", None),
            P("fsdp", "expert", None),
            P("fsdp"),
            P("fsdp", None),
            P("fsdp", None),
            P("fsdp"),
            P("fsdp", None),
            P("fsdp", None),
            P("fsdp"),
            P("fsdp", None),
            P(("expert", "fsdp"), None),
            P(("expert", "fsdp"), None),
            P(("expert", "fsdp"), None),
            P("expert", None, "fsdp"),
            P("expert", None, "fsdp"),
            P("expert", "fsdp", None),
        ),
        out_specs=(
            P("fsdp", "expert", None),
            P("fsdp", "expert", None),
            P("fsdp"),
            P("fsdp", None),
            P("fsdp", None),
            P("fsdp"),
            P("fsdp", None),
            P("fsdp", None),
            P("fsdp"),
            P("fsdp", None),
            P(("expert", "fsdp"), None),
            P(("expert", "fsdp"), None),
            P(("expert", "fsdp"), None),
            P("expert", None, "fsdp"),
            P("expert", None, "fsdp"),
            P("expert", "fsdp", None),
        ),
        check_vma=False,
    )
```

profile of v0, /device:TPU:0, one launch (start us, length us, event | category | flops | bytes accessed | tf_op | source)
XLA Modules:
  0.0 942.1 jit_solution(7279818863445000162)
XLA Ops:
  7.3 3.2 constant_dynamic-slice_fusion.5
  13.4 1.6 constant_dynamic-slice_fusion.8.refs_2_
  14.9 55.0 %shard_map.324 = (bf16[16,128,2048]{2,1,0:T(8,128)(2,1)}, bf16[224,1024]{1,0:T(8,128)(2,1)}, bf16[256,256]{1,0:T(8,128)(2,1)}, bf16[576,1024]{1,0:T(8,128)(2,1)}) custom-call(bf16[128,2048]{1,0:T(8,128)(2,1)} %bitcast.114, bf16[224,1024]{1,0:T(8,128)(2,1)} %pad.38.refs_1_, bf16[256,256]{1,0:T(8,128)(2,1)} %constant_dynamic-slice_fusion.8.refs_2_, ...), custom_call_target="tpu_custom_call" | custom-call | bytes 100663296 | tf_op jit(solution)/shard_map/pallas_call | solution.py:687
  70.9 19.7 %all-gather.4.cloned.1.call-done = bf16[1024,2048]{1,0:T(8,128)(2,1)} async-done(((bf16[512,2048]{1,0:T(8,128)(2,1)}), bf16[1024,2048]{1,0:T(8,128)(2,1)}) %all-gather.4.cloned.1.call-update) | async-done | bytes 4194320 | tf_op jit(solution)/shard_map/all_gather | solution.py:1632
  92.7 4.9 all-to-all-start
  102.6 2.2 pad_maximum_fusion.1.w_front
  105.0 24.8 %shard_map.325 = (bf16[2048,2048]{1,0:T(8,128)(2,1)}, bf16[2048,512]{1,0:T(8,128)(2,1)}, bf16[2048,192]{1,0:T(8,128)(2,1)}, bf16[2048,192]{1,0:T(8,128)(2,1)}, b...) custom-call(bf16[2048,2048]{1,0:T(8,128)(2,1)} %bitcast.157, ...), custom_call_target="tpu_custom_call" | custom-call | flops 8053063680 | bytes 25165824 | tf_op jit(solution)/shard_map/pallas_call | solution.py:1351
  129.8 1.6 copy.46
  133.9 22.8 %shard_map.326 = bf16[16,128,128]{2,1,0:T(8,128)(2,1)} custom-call(bf16[16,128,128]{2,1,0:T(8,128)(2,1)} %bitcast.136), custom_call_target="tpu_custom_call" | custom-call | bytes 10485760 | tf_op jit(solution)/shard_map/pallas_call | solution.py:1156
  158.1 3.1 convolution_add_fusion.2
  161.2 3.0 multiply_reduce_fusion.2
  165.2 113.0 %shard_map.327.normed = bf16[32,128,2048]{2,1,0:T(8,128)(2,1)} custom-call(bf16[128,2048]{1,0:T(8,128)(2,1)} %multiply_convert_fusion.refs_0_), custom_call_target="tpu_custom_call" | custom-call | bytes 201326592 | tf_op jit(solution)/shard_map/pallas_call | solution.py:687
  278.2 3.8 constant_dynamic-slice_fusion
  284.5 103.6 %shard_map.328 = (bf16[32,128,2048]{2,1,0:T(8,128)(2,1)}, bf16[32,128,2176]{2,1,0:T(8,128)(2,1)}, bf16[2048,2048]{1,0:T(8,128)(2,1)}, bf16[2048,2048]{1,0:T(8,12...) custom-call(bf16[32,128,2048]{2,1,0:T(8,128)(2,1)} %shard_map.327.no, ...), custom_call_target="tpu_custom_call" | custom-call | flops 35433480192 | bytes 167772160 | tf_op jit(solution)/shard_map/pallas_call | solution.py:1078
  388.1 99.2 %shard_map.329 = f32[128,2176]{1,0:T(8,128)} custom-call(bf16[32,128,2176]{2,1,0:T(8,128)(2,1)} %get-tuple-element.80.part), custom_call_target="tpu_custom_call" | custom-call | bytes 213909504 | tf_op jit(solution)/shard_map/pallas_call | solution.py:919
  488.0 3.1 multiply_reduce_fusion.5
  493.0 2.4 multiply_reduce_fusion
  498.4 3.7 select_convert_fusion.1
  502.8 1.7 copy.53
  504.5 1.7 copy.57
  511.6 1.9 maximum_bitcast_fusion.x
  513.5 26.3 %shard_map.330 = bf16[16,128,128]{2,1,0:T(8,128)(2,1)} custom-call(bf16[16,128,128]{2,1,0:T(8,128)(2,1)} %maximum_bitcast_fusion.x), custom_call_target="tpu_custom_call" | custom-call | bytes 10485760 | tf_op jit(solution)/shard_map/pallas_call | solution.py:1156
  539.9 19.2 %shard_map.331 = (bf16[2048,192]{1,0:T(8,128)(2,1)}, bf16[2048,256]{1,0:T(8,128)(2,1)}, bf16[2048,640]{1,0:T(8,128)(2,1)}) custom-call(bf16[2048,192]{1,0:T(8,128)(2,1)} %get-tuple-element.73.query, bf16[2048,192]{1,0:T(8,128)(2,1)} %get-tuple-element.74.key, bf16[2048,128]{1,0:T(8,128)(2,1)} %get-tuple-element.75.value, bf16[2048,128]{1,0:T(8,128)(2,1)} %bitcast.137, ...), custom_call_target="tpu_custom_call" | custom-call | flops 4026531840 | bytes 6291456 | tf_op jit(solution)/shard_map/pallas_call | solution.py:1479
  559.1 2.1 convolution_convert_fusion.2
  561.9 5.4 convolution_convert_fusion.1
  569.0 5.7 convolution_convert_fusion
  574.7 130.8 %shard_map.332 = (bf16[16,128,192]{2,1,0:T(8,128)(2,1)}, f32[128,640]{1,0:T(8,128)}, f32[64,2048]{1,0:T(8,128)}, bf16[192,1024]{1,0:T(8,128)(2,1)}, bf16[256,256]{1,0:T(8,128)(2,1)}) custom-call(bf16[16,128,192]{2,1,0:T(8,128)(2,1)} %bitcast.117, bf16[16,128,640]{2,1,0:T(8,128)(2,1)} %bitcast.128, bf16[32,64,2048]{2,1,0:T(8,128)(2,1)} %bitcast.112, ...), custom_call_target="tpu_custom_call" | custom-call | bytes 100663296 | tf_op jit(solution)/shard_map/pallas_call | solution.py:1236
  705.5 1.8 convert_element_type.127.refs_2_
  707.4 1.7 multiply_reduce_fusion.4
  709.6 2.6 copy.58
  716.7 5.5 fusion.73
  722.2 5.1 broadcast_select_fusion.5
  729.0 1.8 fusion.21
  732.0 2.4 pad_maximum_fusion.refs_3_
  735.9 108.0 %shard_map.333 = (bf16[16,192,1024]{2,1,0:T(8,128)(2,1)}, bf16[16,256,256]{2,1,0:T(8,128)(2,1)}, bf16[16,64,2048]{2,1,0:T(8,128)(2,1)}, f32[64,1024]{1,0:T(8,128)}) custom-call(bf16[192,1024]{1,0:T(8,128)(2,1)} %add_convert_fusion.1.refs_0_, bf16[256,256]{1,0:T(8,128)(2,1)} %add_convert_fusion.2.refs_1_, bf16[64,2048]{1,0:T(8,128)(2,1)} %convert_element_type.127.refs_2_, ...), custom_call_target="tpu_custom_call" | custom-call | bytes 150994944 | tf_op jit(solution)/shard_map/pallas_call | solution.py:896
  843.9 1.6 convert_element_type.133.refs_0_
  845.6 23.2 %shard_map.334 = bf16[16,64,1024]{2,1,0:T(8,128)(2,1)} custom-call(bf16[64,1024]{1,0:T(8,128)(2,1)} %convert_element_type.133.refs_0_), custom_call_target="tpu_custom_call" | custom-call | bytes 25165824 | tf_op jit(solution)/shard_map/pallas_call | solution.py:687
  868.8 2.2 convert_element_type.134
  871.0 1.9 slice.176
  874.3 3.4 all-to-all-start.1
  877.7 2.0 slice.156
  879.7 14.4 %shard_map.335 = (f32[1024,3072]{1,0:T(8,128)}, f32[256,4096]{1,0:T(8,128)}, f32[1024,2048]{1,0:T(8,128)}) custom-call(bf16[16,192,1024]{2,1,0:T(8,128)(2,1)} %get-tuple-element.99.query, bf16[16,256,256]{2,1,0:T(8,128)(2,1)} %get-tuple-element.100.expand, bf16[16,64,2048]{2,1,0:T(8,128)(2,1)} %get-tuple-element.101.out_rows), custom_call_target="tpu_custom_call" | custom-call | bytes 18874368 | tf_op jit(solution)/shard_map/pallas_call | solution.py:1530
  894.1 1.6 slice_bitcast_fusion
  896.9 10.4 %convolution_bitcast_fusion = f32[1,704,2048]{2,1,0:T(8,128)} fusion(bf16[2048,704]{1,0:T(8,128)(2,1)S(1)} %copy-done.43, bf16[2048,2048]{1,0:T(8,128)(2,1)} %get-tuple-element.111), kind=kOutput, calls=%fused_computation.8 | convolution fusion | flops 5905580032 | bytes 17039360 | tf_op jit(solution)/shard_map/dot_general | solution.py:28
  907.3 8.3 convolution_bitcast_fusion.2
  917.0 8.4 convolution_bitcast_fusion.1
  930.1 1.8 copy.60
  933.4 1.9 fusion.29
  (194 shorter events, 51.8 us)
Async XLA Ops:
  7.2 83.4 %all-gather.4.cloned.1.call-start = ((), (), s32[]{:S(2)}) async-start(), calls=%async_computation.3 | async-start | bytes 6291456 | tf_op jit(solution)/shard_map/all_gather | solution.py:1632
  7.2 4.9 copy-start.39
  7.3 5.0 copy-start.40
  7.3 5.0 copy-start.42
  7.3 5.0 copy-start.31
  10.5 2.8 copy-start.35
  10.5 274.0 %all-gather.6.cloned.1.call-start = ((), (), s32[]{:S(2)}) async-start(), calls=%async_computation.4 | async-start | bytes 18382848 | tf_op jit(solution)/shard_map/all_gather | solution.py:1556
  10.5 59.4 %copy-start.17 = (bf16[1,128,2048]{2,1,0:T(8,128)(2,1)S(1)}, bf16[1,128,2048]{2,1,0:T(8,128)(2,1)}, u32[]{:S(2)}) copy-start(bf16[1,128,2048]{2,1,0:T(8,128)(2,1)} %param.23) | copy-start | bytes 1572868
  12.2 78.4 %copy-start.25 = (bf16[64,2816]{1,0:T(8,128)(2,1)S(1)}, bf16[64,2816]{1,0:T(8,128)(2,1)}, u32[]{:S(2)}) copy-start(bf16[64,2816]{1,0:T(8,128)(2,1)} %param.33) | copy-start | bytes 1081348
  12.4 78.6 %copy-start.26 = (bf16[64,2816]{1,0:T(8,128)(2,1)S(1)}, bf16[64,2816]{1,0:T(8,128)(2,1)}, u32[]{:S(2)}) copy-start(bf16[64,2816]{1,0:T(8,128)(2,1)} %param.32) | copy-start | bytes 1081348
  70.8 27.0 %copy-start.23 = (bf16[224,1024]{1,0:T(8,128)(2,1)S(1)}, bf16[224,1024]{1,0:T(8,128)(2,1)}, u32[]{:S(2)}) copy-start(bf16[224,1024]{1,0:T(8,128)(2,1)} %get-tuple-element.66) | copy-start | bytes 1376260
  90.6 70.6 %collective-permute-start = (bf16[1024,2048]{1,0:T(8,128)(2,1)}, bf16[1024,2048]{1,0:T(8,128)(2,1)}, u32[]{:S(2)}, u32[]{:S(2)}) collective-permute-start(bf16[1024,2048]{1,0:T(8,128)(2,1)} %all-gather.4.cloned.1.call-done), channel_id=1, source_target_pairs={{0,2},{2,0},{4,6},{6,4},{8,10},{10,8},{12,14},{14,12},{16,18},{18,... | collective-permute-start | bytes 12582920 | tf_op jit(solution)/shard_map/ppermute | solution.py:1634
  91.0 7.7 copy-start.29
  92.7 37.2 %all-to-all-start = ((bf16[32,128,88]{1,2,0:T(8,128)(2,1)}), bf16[32,128,88]{1,2,0:T(8,128)(2,1)}, u32[]{:S(2)}, u32[]{:S(2)}) async-start(bf16[32,128,88]{1,2,0:T(8,128)(2,1)} %bitcast.8), calls=%async_computation | async-start | bytes 1441792 | tf_op jit(solution)/shard_map/all_to_all | solution.py:1662
  97.5 3.5 copy-start.8
  97.5 394.1 %all-gather.8.cloned.1.call-start = ((), (), s32[]{:S(2)}) async-start(), calls=%async_computation.5 | async-start | bytes 9437184 | tf_op jit(solution)/shard_map/all_gather | solution.py:1632
  102.5 2.4 copy-start.11
  132.8 25.3 %copy-start.2 = (bf16[1,128,2048]{2,1,0:T(8,128)(2,1)S(1)}, bf16[1,128,2048]{2,1,0:T(8,128)(2,1)}, u32[]{:S(2)}) copy-start(bf16[1,128,2048]{2,1,0:T(8,128)(2,1)} %param.21) | copy-start | bytes 1572868
  158.0 3.1 copy-start.6
  282.0 651.4 %reduce-scatter.2.cloned.1.call-start = ((), (), s32[]{:S(2)}) async-start(), calls=%async_computation.6 | async-start | bytes 17301504 | tf_op jit(solution)/shard_map/reduce_scatter | solution.py:1741
  487.3 3.8 copy-start.3
  487.5 3.5 copy-start.36
  491.1 216.3 %copy-start.41 = (f32[128]{0:T(128)}, f32[128]{0:T(128)S(1)}, u32[]{:S(2)}) copy-start(f32[128]{0:T(128)S(1)} %add_rsqrt_fusion) | copy-start | bytes 1540
  491.3 4.1 copy-start.33
  491.7 3.8 copy-start.34
  491.7 5.1 copy-start.1
  491.7 230.5 %collective-permute-start.1 = (bf16[1024,3072]{1,0:T(8,128)(2,1)}, bf16[1024,3072]{1,0:T(8,128)(2,1)}, u32[]{:S(2)}, u32[]{:S(2)}) collective-permute-start(bf16[1024,3072]{1,0:T(8,128)(2,1)} %all-gather.8.cloned.1.call-done), channel_id=1, source_target_pairs={{0,2},{2,0},{4,6},{6,4},{8,10},{10,8},{12,14},{14,12},{16,18},{18,... | collective-permute-start | bytes 18874376 | tf_op jit(solution)/shard_map/ppermute | solution.py:1634
  493.0 2.4 copy-start.38
  539.8 19.2 %copy-start.16 = (bf16[2048,512]{1,0:T(8,128)(2,1)S(1)}, bf16[2048,512]{1,0:T(8,128)(2,1)}, u32[]{:S(2)}) copy-start(bf16[2048,512]{1,0:T(8,128)(2,1)} %get-tuple-element.87) | copy-start | bytes 6291460
  559.1 2.8 copy-start.4
  561.2 6.1 copy-start.21
  561.9 7.0 copy-start.7
  574.7 132.7 %copy-start.19 = (f32[128,512]{1,0:T(8,128)S(1)}, f32[128,512]{1,0:T(8,128)}, u32[]{:S(2)}) copy-start(f32[128,512]{1,0:T(8,128)} %get-tuple-element.162) | copy-start | bytes 786436
  705.5 8.0 copy-start.18
  716.7 5.5 copy-start.5
  722.2 5.3 copy-start.37
  731.9 2.4 copy-start.22
  732.0 2.4 copy-start.28
  732.0 3.1 copy-start.15
  732.0 3.1 copy-start.24
  871.0 2.7 copy-start.13
  874.3 51.1 %all-to-all-start.1 = ((bf16[32,64,256]{2,1,0:T(8,128)(2,1)}), bf16[32,64,256]{2,1,0:T(8,128)(2,1)}, u32[]{:S(2)}, u32[]{:S(2)}) async-start(bf16[32,64,256]{2,1,0:T(8,128)(2,1)} %bitcast.134), calls=%async_computation.2 | async-start | bytes 2097152 | tf_op jit(solution)/shard_map/all_to_all | solution.py:1809
  879.7 16.0 %copy-start.20 = (f32[128,2048]{1,0:T(8,128)S(1)}, f32[128,2048]{1,0:T(8,128)}, u32[]{:S(2)}) copy-start(f32[128,2048]{1,0:T(8,128)} %get-tuple-element.163) | copy-start | bytes 3145732
  894.1 2.8 copy-start.43
  895.7 11.5 %slice-start = ((s8[8388608]{0:T(1024)(128)(4,1)}), s8[4194304]{0:T(1024)(128)(4,1)S(1)}, s32[]{:S(2)}) async-start(s8[8388608]{0:T(1024)(128)(4,1)} %bitcast.161), calls=%async_computation.7 | async-start | bytes 8388608
  896.9 10.4 %slice-start.1 = ((s8[8388608]{0:T(1024)(128)(4,1)}), s8[4194304]{0:T(1024)(128)(4,1)S(1)}, s32[]{:S(2)}) async-start(s8[8388608]{0:T(1024)(128)(4,1)} %bitcast.161), calls=%async_computation.8 | async-start | bytes 8388608
  896.9 10.4 %copy-start.45 = (bf16[2048,704]{1,0:T(8,128)(2,1)S(1)}, bf16[2048,704]{1,0:T(8,128)(2,1)}, u32[]{:S(2)}) copy-start(bf16[2048,704]{1,0:T(8,128)(2,1)} %get-tuple-element.108) | copy-start | bytes 8650756
  907.3 9.7 %copy-start.44 = (bf16[2048,704]{1,0:T(8,128)(2,1)S(1)}, bf16[2048,704]{1,0:T(8,128)(2,1)}, u32[]{:S(2)}) copy-start(bf16[2048,704]{1,0:T(8,128)(2,1)} %get-tuple-element.109) | copy-start | bytes 8650756
  (8 other events, 11.8 us)
Sparse Core Ops, SparseCore 0:
  10.6 79.9 all-gather.3
  94.0 168.5 all-gather.5
  282.2 81.7 all-gather.7
  487.4 256.2 reduce-scatter.1
where the time goes:
time: 947 us; the launch traced here: 942 us
  Pallas kernels  740 us (78%)
  matrix products  71.7 us (8%)
  local copies, waits for them, and re-layouts  51.4 us (5%)
  other arithmetic  34.8 us (4%)
  waiting for transfers between devices  19.8 us (2%)
  between operations  15 us (2%)
    pallas_call x3, Pallas kernels, gather_rows(): pl.pallas_call(functools.partial(gather_kernel, full, count, pairs, share...  191 us
    pallas_call x1, Pallas kernels, exchange_and_sums(): pl.pallas_call(functools.partial(sums_kernel, pairs), out_shape=[jax.Shap...  131 us
    pallas_call x1, Pallas kernels, gather_and_scatter(): pl.pallas_call(functools.partial(gather_scatter_kernel, count, gated), ou...  108 us
    pallas_call x1, Pallas kernels, expert_phase(): pl.pallas_call(functools.partial(expert_kernel, capacity), grid=(blocks /...  104 us
    pallas_call x1, Pallas kernels, scatter_rows(): pl.pallas_call(functools.partial(scatter_kernel, full, pairs), out_shape=...  99.2 us
    pallas_call x2, Pallas kernels, exchange(): pl.pallas_call(exchange_kernel, out_shape=jax.ShapeDtypeStruct(x.shape, x...  49.1 us
    dot_general x8, matrix products, inner(): lax.dot_general(left, right, (((0,), (0,)), ((), ())), preferred_element_...  42.3 us
    pallas_call x1, Pallas kernels, attend(): pl.pallas_call(attend_kernel, grid=(steps,), out_shape=[jax.ShapeDtypeStr...  24.8 us
  transfers between devices with their start and end apart: 8, of which 1 were waited for; matrix products, arithmetic and copies ran while one was open for 16% of the time, Pallas kernels for 79%

commit v1 on v0

--- a/solution.py
+++ b/solution.py
@@ -1514,6 +1514,148 @@
     )(query, key, value, d_head, head_sum, logs, expand_head, cosines, sines)
 
 
+def norm_back_rows(value, gain, grad):
+    inverse = lax.rsqrt(jnp.mean(value * value, axis=-1, keepdims=True) + EPS)
+    unit = value * inverse
+    scaled = grad * gain
+    d_value = inverse * (scaled - unit * jnp.mean(scaled * unit, axis=-1, keepdims=True))
+    return d_value, jnp.sum(grad * unit, axis=0, keepdims=True)
+
+
+def hidden_back_kernel(
+    d_back,
+    router,
+    normed,
+    hidden,
+    gain,
+    router_rows,
+    grads,
+    out_own,
+    out_other,
+    d_hidden_out,
+    d_attn_out,
+    d_heads_out,
+    g_router_out,
+    g_gain_out,
+):
+    bf16 = jnp.bfloat16
+    width = hidden.shape[1]
+    spare = router.shape[1]
+    gates = router[...]
+    d_router = d_back[:, width : width + spare]
+    d_logits = gates * (d_router - jnp.sum(gates * d_router, axis=1, keepdims=True))
+    d_logits = d_logits.astype(bf16)
+    g_router_out[...] = contract_first(d_logits, normed[...])
+    d_normed = d_back[:, :width] + matrix_product(d_logits, router_rows[...])
+    d_value, g_gain = norm_back_rows(hidden[...], gain[...], d_normed)
+    g_gain_out[...] = g_gain
+    d_hidden = grads[...].astype(jnp.float32) + d_value
+    d_hidden_out[...] = d_hidden
+    d_attn = d_hidden.astype(bf16)
+    d_attn_out[...] = d_attn
+    shard = lax.axis_index("fsdp")
+    half = out_own.shape[0] // VALUE_UNITS
+    for weight, first in ((out_own, shard * half), (out_other, (1 - shard) * half)):
+        product = contract_last(d_attn, weight[...]).astype(bf16)
+        for at in range(half):
+            d_heads_out[first + at] = product[:, at * VALUE_UNITS : (at + 1) * VALUE_UNITS]
+
+
+def hidden_back(d_back, router, normed, hidden, gain, router_rows, grads, out_own, out_other):
+    rows, width = hidden.shape
+    heads = 2 * out_own.shape[0] // VALUE_UNITS
+    return pl.pallas_call(
+        hidden_back_kernel,
+        out_shape=[
+            jax.ShapeDtypeStruct((rows, width), jnp.float32),
+            jax.ShapeDtypeStruct((rows, width), jnp.bfloat16),
+            jax.ShapeDtypeStruct((heads, rows, VALUE_UNITS), jnp.bfloat16),
+            jax.ShapeDtypeStruct((router.shape[1], width), jnp.float32),
+            jax.ShapeDtypeStruct((1, width), jnp.float32),
+        ],
+        compiler_params=pltpu.CompilerParams(vmem_limit_bytes=VMEM_LIMIT),
+        cost_estimate=pl.CostEstimate(
+            flops=4 * rows * width * out_own.shape[0],
+            bytes_accessed=4 * out_own.size + 16 * rows * width,
+            transcendentals=0,
+        ),
+    )(d_back, router, normed, hidden, gain, router_rows, grads, out_own, out_other)
+
+
+def input_back_kernel(
+    d_query,
+    d_sums,
+    query_own,
+    query_other,
+    tokens,
+    gain,
+    w_latent,
+    lat_gain,
+    cosines,
+    sines,
+    d_hidden,
+    d_tokens_out,
+    g_latent_out,
+    g_gain_out,
+    g_lat_out,
+):
+    bf16 = jnp.bfloat16
+    x = tokens[...].astype(jnp.float32)
+    normed, _ = norm_forward(x, gain[...])
+    normed = normed.astype(bf16)
+    latent = contract_last(normed, w_latent[:LATENT_WIDTH, :])
+    d_compact, g_lat = norm_back_rows(latent, lat_gain[...], d_sums[:, :LATENT_WIDTH])
+    g_lat_out[...] = g_lat
+    d_rope = d_sums[:, LATENT_WIDTH : LATENT_WIDTH + ROTARY_UNITS]
+    d_rope = d_rope * cosines[...] - swap_halves(d_rope) * sines[...]
+    d_latent = jnp.concatenate([d_compact, d_rope], axis=1).astype(bf16)
+    g_latent_out[...] = contract_first(d_latent, normed)
+    d_full = jnp.concatenate([d_query[at] for at in range(d_query.shape[0])], axis=1)
+    own = contract_last(d_full, query_own[...])
+    other = contract_last(d_full, query_other[...])
+    first = lax.rem(lax.axis_index("expert"), CORES) == 0
+    lower, upper = jnp.where(first, own, other), jnp.where(first, other, own)
+    size = lower.shape[1] // 2
+    d_normed = jnp.concatenate(
+        [lower[:, :size], upper[:, :size], lower[:, size:], upper[:, size:]], axis=1
+    )
+    d_normed = d_normed + matrix_product(d_latent, w_latent[...])
+    d_value, g_gain = norm_back_rows(x, gain[...], d_normed)
+    g_gain_out[...] = g_gain
+    d_tokens_out[...] = (d_hidden[...] + d_value).astype(bf16)
+
+
+def input_back(d_query, d_sums, query_own, query_other, tokens, gain, w_latent, lat_gain, cosines, sines, d_hidden):
+    rows, width = tokens.shape
+    return pl.pallas_call(
+        input_back_kernel,
+        out_shape=[
+            jax.ShapeDtypeStruct((rows, width), jnp.bfloat16),
+            jax.ShapeDtypeStruct((w_latent.shape[0], width), jnp.float32),
+            jax.ShapeDtypeStruct((1, width), jnp.float32),
+            jax.ShapeDtypeStruct((1, LATENT_WIDTH), jnp.float32),
+        ],
+        compiler_params=pltpu.CompilerParams(vmem_limit_bytes=VMEM_LIMIT),
+        cost_estimate=pl.CostEstimate(
+            flops=4 * rows * query_own.size,
+            bytes_accessed=4 * query_own.size + 16 * rows * width,
+            transcendentals=0,
+        ),
+    )(
+        d_query,
+        d_sums,
+        query_own,
+        query_other,
+        tokens,
+        gain,
+        w_latent,
+        lat_gain,
+        cosines,
+        sines,
+        d_hidden,
+    )
+
+
 def finish_kernel(query, expand, out_rows, query_out, expand_out, out_out):
     heads, units, width = query.shape
     query_out[...] = query[...].reshape(heads * units, width).astype(jnp.float32).T
@@ -1599,8 +1741,8 @@
         axis=0,
     )
     packed = jnp.pad(packed, ((0, -packed.shape[0] % 32), (0, 0)))
-    seq_rows, other_packed, other_expand, other_latent = gather_rows(
-        [tokens[0]], False, 0, swapped=[packed, expand_cols], halved=[latent_weight.T]
+    seq_rows, other_packed, other_expand, other_latent, out_other = gather_rows(
+        [tokens[0]], False, 0, swapped=[packed, expand_cols], halved=[latent_weight.T, w_out]
     )
 
     def whole(own, other, axis):
@@ -1633,29 +1775,12 @@
         swap = [(index, index ^ 1) for index in range(experts)]
         return own, lax.ppermute(own, "expert", swap)
 
-    def core_columns(value, which):
-        size = value.shape[1] // (CORES * shards)
-        parts = [
-            lax.dynamic_slice_in_dim(value, (at * CORES + which) * size, size, 1)
-            for at in range(shards)
-        ]
-        return jnp.concatenate(parts, axis=1)
-
-    def in_order(own, other):
-        lower, upper = jnp.where(core == 0, own, other), jnp.where(core == 0, other, own)
-        size = own.shape[1] // shards
-        parts = []
-        for at in range(shards):
-            parts += [lower[:, at * size : (at + 1) * size], upper[:, at * size : (at + 1) * size]]
-        return jnp.concatenate(parts, axis=1)
-
-    out_own, out_other = by_cores(w_out)
     grad_rows = cotangent[0]
     grad_out = grad_rows.astype(jnp.float32)
     own_routes = jnp.pad(routes[0], ((0, 0), (0, 128 - TOPK)), constant_values=-1)
     grad_rows = jnp.concatenate([grad_rows, own_routes.astype(jnp.bfloat16)], axis=1)
-    seq_rows, grad_rows, shared_gate, shared_up = lax.optimization_barrier(
-        (seq_rows, grad_rows, shared_gate, shared_up)
+    seq_rows, shared_gate, shared_up = lax.optimization_barrier(
+        (seq_rows, shared_gate, shared_up)
     )
     def to_columns(weight):
         parts = weight.reshape(weight.shape[0], blocks, units).transpose(1, 0, 2)
@@ -1703,8 +1828,10 @@
     head_rows, shared_in = lax.optimization_barrier((head_rows, shared_in))
     heads = exchange(head_rows.reshape(experts, rows, VALUE_UNITS), 1)
     heads = heads.transpose(1, 0, 2).reshape(rows, experts * VALUE_UNITS)
-    hidden = x_in + matrix_product(core_columns(heads, core), out_own)
-    hidden = hidden + matrix_product(core_columns(heads, 1 - core), out_other)
+    half_heads = w_out.shape[0]
+    own_heads = lax.dynamic_slice_in_dim(heads, shard * half_heads, half_heads, 1)
+    other_heads = lax.dynamic_slice_in_dim(heads, (1 - shard) * half_heads, half_heads, 1)
+    hidden = x_in + matrix_product(own_heads, w_out) + matrix_product(other_heads, out_other)
     normed2, inv_ffn = norm_forward(hidden, g_ffn)
     normed_ffn = normed2.astype(jnp.bfloat16)
     router = jax.nn.softmax(outer_product(normed_ffn, wrout), axis=-1)
@@ -1744,21 +1871,19 @@
         scatter_dimension=0,
         tiled=True,
     )
-    d_normed_ffn = d_back[:, :MODEL_WIDTH]
-    d_router = d_back[:, MODEL_WIDTH : MODEL_WIDTH + experts]
-
-    d_logits = (router * (d_router - jnp.sum(router * d_router, axis=1, keepdims=True))).astype(
-        jnp.bfloat16
-    )
-    g_router = inner(d_logits, normed_ffn)
-    d_normed_ffn = d_normed_ffn + matrix_product(d_logits, wrout)
-    d_hidden_norm, g_ffn_grad = norm_backward(hidden, inv_ffn, g_ffn, d_normed_ffn)
-    d_hidden = grad_out + d_hidden_norm
-    d_attn = d_hidden.astype(jnp.bfloat16)
-
-    d_heads = in_order(outer_product(d_attn, out_own), outer_product(d_attn, out_other))
-    d_heads = d_heads.astype(jnp.bfloat16)
-    d_heads = d_heads.reshape(rows, experts, VALUE_UNITS).transpose(1, 0, 2)
+    spare = router_rows.shape[0]
+    d_hidden, d_attn, d_heads, g_router, g_ffn_grad = hidden_back(
+        d_back,
+        jnp.pad(router, ((0, 0), (0, spare - experts))),
+        normed_ffn,
+        hidden,
+        g_ffn[None],
+        router_rows,
+        cotangent[0],
+        w_out,
+        out_other,
+    )
+    g_router = g_router[:experts]
     d_head = exchange(d_heads, 4).reshape(seq_len, VALUE_UNITS)
     out_grad_part = inner(heads, d_attn).astype(jnp.bfloat16)
     d_query_full, d_pairs, d_keys = attend_back(
@@ -1779,31 +1904,27 @@
         [half_of(g_query_head, 1 - shard, 1), half_of(g_expand_head, 1 - shard, 0)],
         5,
     )
-    own_d_query = own_d_query.transpose(1, 0, 2).reshape(rows, experts * head_units)
-    key_gradient = d_sums[:, :feature_width]
-    d_normed_in = in_order(
-        outer_product(own_d_query, query_own), outer_product(own_d_query, query_other)
-    )
-
     def summed(own, other):
         return (own.astype(jnp.float32) + other.astype(jnp.float32)).astype(jnp.bfloat16)
 
     own_query = summed(half_of(g_query_head, shard, 1), other_query)
     own_expand = summed(half_of(g_expand_head, shard, 0), other_expand)
     own_out = own_out.astype(jnp.bfloat16)
-    own_latent = outer_product(normed_in, w_latent[:LATENT_WIDTH])
-    own_cosine = lax.dynamic_slice_in_dim(cosine_table, position * rows, rows, 0)
-    own_sine = lax.dynamic_slice_in_dim(sine_table, position * rows, rows, 0)
-    inv_lat = lax.rsqrt(jnp.mean(own_latent * own_latent, axis=-1, keepdims=True) + EPS)
-    d_compact, g_lat_grad = norm_backward(
-        own_latent, inv_lat, g_lat, key_gradient[:, :LATENT_WIDTH]
-    )
-    d_rope = reverse_rotary(key_gradient[:, LATENT_WIDTH:], own_cosine, own_sine)
-    d_latent_full = jnp.concatenate([d_compact, d_rope], axis=-1).astype(jnp.bfloat16)
-    g_latent = inner(d_latent_full, normed_in)
-    d_normed_in = d_normed_in + matrix_product(d_latent_full, w_latent)
-    d_norm_in, g_attn_grad = norm_backward(x_in, inv_attn, g_attn, d_normed_in)
-    d_tokens = (d_hidden + d_norm_in).astype(jnp.bfloat16)
+    own_cosines = lax.dynamic_slice_in_dim(cosines, position * rows, rows, 0)
+    own_sines = lax.dynamic_slice_in_dim(sines, position * rows, rows, 0)
+    d_tokens, g_latent, g_attn_grad, g_lat_grad = input_back(
+        own_d_query,
+        d_sums,
+        query_own,
+        query_other,
+        tokens[0],
+        g_attn[None],
+        w_latent,
+        g_lat[None],
+        own_cosines,
+        own_sines,
+        d_hidden,
+    )
 
     half = MODEL_WIDTH // blocks
     cols = lax.all_to_all(
@@ -1818,14 +1939,14 @@
     r_sup = cols[:, :, lanes : lanes + units].reshape(half, blocks * units)
     g_sdown = g_shared_out[:units]
     model_half = MODEL_WIDTH // shards
-    small_rows = jnp.concatenate([g_latent, g_router, g_attn_grad[None], g_ffn_grad[None]], axis=0)
+    small_rows = jnp.concatenate([g_latent, g_router, g_attn_grad, g_ffn_grad], axis=0)
     used = small_rows.shape[0]
     share = 2 * 32 * (-(-(used + 1) // (2 * 32 * experts)))
 
     def rows_for(which):
         here = small_rows[:, which * model_half : (which + 1) * model_half]
         lat = jnp.pad(
-            g_lat_grad[which * lat_half : (which + 1) * lat_half], (0, model_half - lat_half)
+            g_lat_grad[0, which * lat_half : (which + 1) * lat_half], (0, model_half - lat_half)
         )
         full = jnp.concatenate([here, lat[None]], axis=0).astype(jnp.bfloat16)
         full = jnp.pad(full, ((0, experts * share - used - 1), (0, 0)))

time: 947 us -> 915 us (0.966)
  Pallas kernels: 740 us -> 771 us
  matrix products: 71.7 us -> 47.6 us
  local copies, waits for them, and re-layouts: 51.4 us -> 33.3 us
  waiting for transfers between devices: 19.8 us -> 6.27 us
    pallas_call x0 -> x2, Pallas kernels: none -> 22.7 us  [the longest x1 13.9 us: input_back(): pl.pallas_call(input_back_kernel, out_shape=[jax.ShapeDtypeStruct((rows,...]
    all_gather x2 -> x1, waiting for transfers between devices: 19.7 us -> 0.02 us  [by_cores(): own = lax.all_gather(own, 'fsdp', axis=0, tiled=True)]
    dot_general x6 -> x1, matrix products: 19.1 us -> 0.25 us  [outer_product(): lax.dot_general(left, right, (((1,), (1,)), ((), ())), preferred_element_...]
    pallas_call x2, Pallas kernels: 49.1 us -> 37.1 us  [exchange(): pl.pallas_call(exchange_kernel, out_shape=jax.ShapeDtypeStruct(x.shape, x...]
    pallas_call x1, Pallas kernels: 108 us -> 120 us  [gather_and_scatter(): pl.pallas_call(functools.partial(gather_scatter_kernel, count, gated), ou...]
    dot_general x8 -> x6, matrix products: 42.3 us -> 42.4 us  [inner(): lax.dot_general(left, right, (((0,), (0,)), ((), ())), preferred_element_...]
  transfers between devices with their start and end apart: 8 -> 6, of which waited for: 1 -> 1; matrix products, arithmetic and copies ran while one was open for 16% -> 11% of each run, Pallas kernels for 79% -> 85%
where the time goes in v1:
time: 915 us; the launch traced here: 911 us
  Pallas kernels  771 us (84%)
  matrix products  47.6 us (5%)
  local copies, waits for them, and re-layouts  33.3 us (4%)
  other arithmetic  29.2 us (3%)
  between operations  14.7 us (2%)
    pallas_call x3, Pallas kernels, gather_rows(): pl.pallas_call(functools.partial(gather_kernel, full, count, pairs, share...  200 us
    pallas_call x1, Pallas kernels, exchange_and_sums(): pl.pallas_call(functools.partial(sums_kernel, pairs), out_shape=[jax.Shap...  132 us
    pallas_call x1, Pallas kernels, gather_and_scatter(): pl.pallas_call(functools.partial(gather_scatter_kernel, count, gated), ou...  120 us
    pallas_call x1, Pallas kernels, expert_phase(): pl.pallas_call(functools.partial(expert_kernel, capacity), grid=(blocks /...  105 us
    pallas_call x1, Pallas kernels, scatter_rows(): pl.pallas_call(functools.partial(scatter_kernel, full, pairs), out_shape=...  97.3 us
    dot_general x6, matrix products, inner(): lax.dot_general(left, right, (((0,), (0,)), ((), ())), preferred_element_...  42.4 us
    pallas_call x2, Pallas kernels, exchange(): pl.pallas_call(exchange_kernel, out_shape=jax.ShapeDtypeStruct(x.shape, x...  37.1 us
    pallas_call x1, Pallas kernels, attend(): pl.pallas_call(attend_kernel, grid=(steps,), out_shape=[jax.ShapeDtypeStr...  24.8 us
  transfers between devices with their start and end apart: 6, of which 1 were waited for; matrix products, arithmetic and copies ran while one was open for 11% of the time, Pallas kernels for 85%

profile of v1, /device:TPU:0, one launch (start us, length us, event | category | flops | bytes accessed | tf_op | source)
XLA Modules:
  0.0 911.0 jit_solution(6192652594179353876)
XLA Ops:
  8.1 1.9 fusion.8
  10.0 1.4 constant_dynamic-slice_fusion.6
  12.6 1.6 constant_dynamic-slice_fusion.5.refs_2_
  14.2 95.2 %shard_map.306 = (bf16[16,128,2048]{2,1,0:T(8,128)(2,1)}, bf16[224,1024]{1,0:T(8,128)(2,1)}, bf16[256,256]{1,0:T(8,128)(2,1)}, bf16[576,1024]{1,0:T(8,128)(2,1)}, bf16[1024,2048]{1,0:T(8,128)(2,1)}) custom-call(bf16[128,2048]{1,0:T(8,128)(2,1)} %bitcast.86, bf16[224,1024]{1,0:T(8,128)(2,1)} %pad.42.refs_1_, ...), custom_call_target="tpu_custom_call" | custom-call | bytes 100663296 | tf_op jit(solution)/shard_map/pallas_call | solution.py:687
  110.1 1.3 pad_maximum_fusion.3
  111.4 5.3 all-to-all-start
  117.0 1.3 broadcast_select_fusion.3
  121.3 1.4 broadcast_select_fusion.1
  122.8 2.0 pad_maximum_fusion.1.w_front
  124.8 24.8 %shard_map.307 = (bf16[2048,2048]{1,0:T(8,128)(2,1)}, bf16[2048,512]{1,0:T(8,128)(2,1)}, bf16[2048,192]{1,0:T(8,128)(2,1)}, bf16[2048,192]{1,0:T(8,128)(2,1)}, b...) custom-call(bf16[2048,2048]{1,0:T(8,128)(2,1)} %bitcast.109, ...), custom_call_target="tpu_custom_call" | custom-call | flops 8053063680 | bytes 25165824 | tf_op jit(solution)/shard_map/pallas_call | solution.py:1351
  149.7 6.2 all-to-all-done
  155.8 1.6 copy.53
  158.8 1.1 copy.64
  159.9 12.3 %shard_map.308 = bf16[16,128,128]{2,1,0:T(8,128)(2,1)} custom-call(bf16[16,128,128]{2,1,0:T(8,128)(2,1)} %bitcast.100), custom_call_target="tpu_custom_call" | custom-call | bytes 10485760 | tf_op jit(solution)/shard_map/pallas_call | solution.py:1156
  172.2 1.3 copy.55
  173.6 3.2 convolution_add_fusion.1
  177.2 1.8 multiply_reduce_fusion
  180.1 77.8 %shard_map.309.normed = bf16[32,128,2048]{2,1,0:T(8,128)(2,1)} custom-call(bf16[128,2048]{1,0:T(8,128)(2,1)} %multiply_convert_fusion.refs_0_.normed), custom_call_target="tpu_custom_call" | custom-call | bytes 201326592 | tf_op jit(solution)/shard_map/pallas_call | solution.py:687
  258.0 3.8 constant_dynamic-slice_fusion.2
  264.2 104.5 %shard_map.310 = (bf16[32,128,2048]{2,1,0:T(8,128)(2,1)}, bf16[32,128,2176]{2,1,0:T(8,128)(2,1)}, bf16[2048,2048]{1,0:T(8,128)(2,1)}, bf16[2048,2048]{1,0:T(8,12...) custom-call(bf16[32,128,2048]{2,1,0:T(8,128)(2,1)} %shard_map.309.no, ...), custom_call_target="tpu_custom_call" | custom-call | flops 35433480192 | bytes 167772160 | tf_op jit(solution)/shard_map/pallas_call | solution.py:1078
  368.7 97.3 %shard_map.311.d_back = f32[128,2176]{1,0:T(8,128)} custom-call(bf16[32,128,2176]{2,1,0:T(8,128)(2,1)} %get-tuple-element.89.part), custom_call_target="tpu_custom_call" | custom-call | bytes 213909504 | tf_op jit(solution)/shard_map/pallas_call | solution.py:919
  466.2 1.6 constant_dynamic-slice_fusion
  467.8 1.6 pad_maximum_fusion.2.w_latent
  470.7 8.8 shard_map.312
  479.5 24.8 %shard_map.313 = bf16[16,128,128]{2,1,0:T(8,128)(2,1)} custom-call(bf16[16,128,128]{2,1,0:T(8,128)(2,1)} %get-tuple-element.91.x), custom_call_target="tpu_custom_call" | custom-call | bytes 10485760 | tf_op jit(solution)/shard_map/pallas_call | solution.py:1156
  505.3 19.3 %shard_map.314 = (bf16[2048,192]{1,0:T(8,128)(2,1)}, bf16[2048,256]{1,0:T(8,128)(2,1)}, bf16[2048,640]{1,0:T(8,128)(2,1)}) custom-call(bf16[2048,192]{1,0:T(8,128)(2,1)} %get-tuple-element.83.query, bf16[2048,192]{1,0:T(8,128)(2,1)} %get-tuple-element.84.key, bf16[2048,128]{1,0:T(8,128)(2,1)} %get-tuple-element.85.value, bf16[2048,128]{1,0:T(8,128)(2,1)} %bitcast.101, ...), custom_call_target="tpu_custom_call" | custom-call | flops 4026531840 | bytes 6291456 | tf_op jit(solution)/shard_map/pallas_call | solution.py:1479
  524.6 2.1 convolution_convert_fusion.2
  527.4 5.4 convolution_convert_fusion.1
  533.5 5.7 convolution_convert_fusion
  539.3 131.7 %shard_map.315 = (bf16[16,128,192]{2,1,0:T(8,128)(2,1)}, f32[128,640]{1,0:T(8,128)}, f32[64,2048]{1,0:T(8,128)}, bf16[192,1024]{1,0:T(8,128)(2,1)}, bf16[256,256]{1,0:T(8,128)(2,1)}) custom-call(bf16[16,128,192]{2,1,0:T(8,128)(2,1)} %bitcast.81, bf16[16,128,640]{2,1,0:T(8,128)(2,1)} %bitcast.93, bf16[32,64,2048]{2,1,0:T(8,128)(2,1)} %bitcast.77, ...), custom_call_target="tpu_custom_call" | custom-call | bytes 100663296 | tf_op jit(solution)/shard_map/pallas_call | solution.py:1236
  671.0 13.9 %shard_map.316 = (bf16[128,2048]{1,0:T(8,128)(2,1)}, f32[576,2048]{1,0:T(8,128)}, f32[1,2048]{1,0:T(1,128)}, f32[1,512]{1,0:T(1,128)}) custom-call(bf16[16,128,192]{2,1,0:T(8,128)(2,1)} %get-tuple-element.103.d_query, f32[128,640]{1,0:T(8,128)} %get-tuple-element.104.d_sums, bf16[1024,3072]{1,0:T(8,128)(2,1)} %all-gather.5.cloned.1.call-done.query_own, ...), custom_call_target="tpu_custom_call" | custom-call | flops 1610612736 | bytes 16777216 | tf_op jit(solution)/shard_map/pallas_call | solution.py:1630
  686.3 2.7 maximum_convert_fusion
  689.9 2.4 pad_maximum_fusion.refs_3_
  693.8 119.8 %shard_map.317 = (bf16[16,192,1024]{2,1,0:T(8,128)(2,1)}, bf16[16,256,256]{2,1,0:T(8,128)(2,1)}, bf16[16,64,2048]{2,1,0:T(8,128)(2,1)}, f32[64,1024]{1,0:T(8,128)}) custom-call(bf16[192,1024]{1,0:T(8,128)(2,1)} %add_convert_fusion.1.refs_0_, bf16[256,256]{1,0:T(8,128)(2,1)} %add_convert_fusion.2.refs_1_, bf16[64,2048]{1,0:T(8,128)(2,1)} %convert_element_type.108.refs_2_, ...), custom_call_target="tpu_custom_call" | custom-call | bytes 150994944 | tf_op jit(solution)/shard_map/pallas_call | solution.py:896
  813.6 1.6 convert_element_type.111.refs_0_
  815.2 26.8 %shard_map.318 = bf16[16,64,1024]{2,1,0:T(8,128)(2,1)} custom-call(bf16[64,1024]{1,0:T(8,128)(2,1)} %convert_element_type.111.refs_0_), custom_call_target="tpu_custom_call" | custom-call | bytes 25165824 | tf_op jit(solution)/shard_map/pallas_call | solution.py:687
  842.0 2.2 convert_element_type.112
  844.3 1.7 slice.108
  847.6 2.6 all-to-all-start.1
  851.1 14.4 %shard_map.319 = (f32[1024,3072]{1,0:T(8,128)}, f32[256,4096]{1,0:T(8,128)}, f32[1024,2048]{1,0:T(8,128)}) custom-call(bf16[16,192,1024]{2,1,0:T(8,128)(2,1)} %get-tuple-element.117.query, bf16[16,256,256]{2,1,0:T(8,128)(2,1)} %get-tuple-element.118.expand, bf16[16,64,2048]{2,1,0:T(8,128)(2,1)} %get-tuple-element.119.out_rows), custom_call_target="tpu_custom_call" | custom-call | bytes 18874368 | tf_op jit(solution)/shard_map/pallas_call | solution.py:1672
  865.6 1.5 slice_bitcast_fusion
  867.0 10.3 %convolution_bitcast_fusion = f32[1,704,2048]{2,1,0:T(8,128)} fusion(bf16[2048,704]{1,0:T(8,128)(2,1)S(1)} %copy-done.29, bf16[2048,2048]{1,0:T(8,128)(2,1)} %get-tuple-element.129), kind=kOutput, calls=%fused_computation.8 | convolution fusion | flops 5905580032 | bytes 17039360 | tf_op jit(solution)/shard_map/dot_general | solution.py:28
  877.4 10.5 %convolution_bitcast_fusion.1 = f32[1,2048,704]{1,2,0:T(8,128)} fusion(bf16[2048,2048]{1,0:T(8,128)(2,1)} %get-tuple-element.125, bf16[2048,704]{1,0:T(8,128)(2,1)S(1)} %copy-done.31), kind=kOutput, calls=%fused_computation.9 | convolution fusion | flops 5905580032 | bytes 17039360 | tf_op jit(solution)/shard_map/dot_general | solution.py:28
  887.9 1.4 fusion.22
  889.3 8.5 convolution_bitcast_fusion.2
  898.9 1.4 reshape.134
  900.9 1.4 reshape.135
  902.3 1.9 fusion.9
  (131 shorter events, 23.2 us)
Async XLA Ops:
  7.2 4.4 copy-start.28
  7.2 4.4 copy-start.26
  7.2 4.4 copy-start.27
  7.2 4.4 copy-start.24
  7.2 257.0 %all-gather.3.cloned.1.call-start = ((), (), s32[]{:S(2)}) async-start(), calls=%async_computation.3 | async-start | bytes 18382848 | tf_op jit(solution)/shard_map/all_gather | solution.py:1698
  14.2 95.2 %copy-start.18 = (bf16[64,2816]{1,0:T(8,128)(2,1)S(1)}, bf16[64,2816]{1,0:T(8,128)(2,1)}, u32[]{:S(2)}) copy-start(bf16[64,2816]{1,0:T(8,128)(2,1)} %param.30) | copy-start | bytes 1081348
  14.2 95.6 %copy-start.19 = (bf16[64,2816]{1,0:T(8,128)(2,1)S(1)}, bf16[64,2816]{1,0:T(8,128)(2,1)}, u32[]{:S(2)}) copy-start(bf16[64,2816]{1,0:T(8,128)(2,1)} %param.31) | copy-start | bytes 1081348
  109.7 9.2 %copy-start.22 = (bf16[256,256]{1,0:T(8,128)(2,1)S(1)}, bf16[256,256]{1,0:T(8,128)(2,1)}, u32[]{:S(2)}) copy-start(bf16[256,256]{1,0:T(8,128)(2,1)} %get-tuple-element.77) | copy-start | bytes 393220
  111.4 44.5 %all-to-all-start = ((bf16[32,128,88]{1,2,0:T(8,128)(2,1)}), bf16[32,128,88]{1,2,0:T(8,128)(2,1)}, u32[]{:S(2)}, u32[]{:S(2)}) async-start(bf16[32,128,88]{1,2,0:T(8,128)(2,1)} %bitcast.6), calls=%async_computation | async-start | bytes 1441792 | tf_op jit(solution)/shard_map/all_to_all | solution.py:1787
  116.7 4.6 copy-start.10
  116.7 349.3 %all-gather.5.cloned.1.call-start = ((), (), s32[]{:S(2)}) async-start(), calls=%async_computation.4 | async-start | bytes 9437184 | tf_op jit(solution)/shard_map/all_gather | solution.py:1774
  121.2 57.8 %copy-start.23 = (f32[1,2048]{1,0:T(1,128)}, f32[1,2048]{1,0:T(1,128)S(1)}, u32[]{:S(2)}) copy-start(f32[1,2048]{1,0:T(1,128)S(1)} %get-tuple-element.140.gain) | copy-start | bytes 24580
  122.8 2.1 copy-start.4
  157.7 15.9 %copy-start.11 = (bf16[1,128,2048]{2,1,0:T(8,128)(2,1)S(1)}, bf16[1,128,2048]{2,1,0:T(8,128)(2,1)}, u32[]{:S(2)}) copy-start(bf16[1,128,2048]{2,1,0:T(8,128)(2,1)} %param.19) | copy-start | bytes 1572868
  173.6 3.2 copy-start.8
  173.6 3.6 copy-start.1
  179.0 79.0 %copy-start.2 = (f32[128,2048]{1,0:T(8,128)}, f32[128,2048]{1,0:T(8,128)S(1)}, u32[]{:S(2)}) copy-start(f32[128,2048]{1,0:T(8,128)S(1)} %get-tuple-element.113.hidden) | copy-start | bytes 3145732
  261.7 1.0 copy-start.20
  261.8 640.6 %reduce-scatter.2.cloned.1.call-start = ((), (), s32[]{:S(2)}) async-start(), calls=%async_computation.5 | async-start | bytes 17301504 | tf_op jit(solution)/shard_map/reduce_scatter | solution.py:1868
  466.0 1.8 copy-start.5
  466.1 204.9 %collective-permute-start = (bf16[1024,3072]{1,0:T(8,128)(2,1)}, bf16[1024,3072]{1,0:T(8,128)(2,1)}, u32[]{:S(2)}, u32[]{:S(2)}) collective-permute-start(bf16[1024,3072]{1,0:T(8,128)(2,1)} %all-gather.5.cloned.1.call-done.query_own), channel_id=1, source_target_pairs={{0,2},{2,0},{4,6},{6,4},{8,10},{10,8},{12,14},{14,12},{16,18},{18,... | collective-permute-start | bytes 18874376 | tf_op jit(solution)/shard_map/ppermute | solution.py:1776
  466.1 3.3 copy-start.6
  505.3 19.3 %copy-start.13 = (bf16[2048,512]{1,0:T(8,128)(2,1)S(1)}, bf16[2048,512]{1,0:T(8,128)(2,1)}, u32[]{:S(2)}) copy-start(bf16[2048,512]{1,0:T(8,128)(2,1)} %get-tuple-element.98) | copy-start | bytes 6291460
  524.6 2.8 copy-start.7
  527.4 6.2 copy-start.9
  527.4 6.2 copy-start.15
  671.0 14.6 %copy-start.14 = (f32[64,2048]{1,0:T(8,128)S(1)}, f32[64,2048]{1,0:T(8,128)}, u32[]{:S(2)}) copy-start(f32[64,2048]{1,0:T(8,128)} %get-tuple-element.102) | copy-start | bytes 1572868
  671.0 15.4 %copy-start.25 = (f32[1,2048]{1,0:T(1,128)S(1)}, f32[1,2048]{1,0:T(1,128)}, u32[]{:S(2)}) copy-start(f32[1,2048]{1,0:T(1,128)} %get-tuple-element.110) | copy-start | bytes 24580
  689.8 2.4 copy-start.21
  689.9 3.1 copy-start.17
  842.0 2.2 copy-start
  844.3 2.7 copy-start.12
  844.3 5.9 copy-start.16
  847.6 50.2 %all-to-all-start.1 = ((bf16[32,64,256]{2,1,0:T(8,128)(2,1)}), bf16[32,64,256]{2,1,0:T(8,128)(2,1)S(1)}, u32[]{:S(2)}, u32[]{:S(2)}) async-start(bf16[32,64,256]{2,1,0:T(8,128)(2,1)} %bitcast.37), calls=%async_computation.2 | async-start | bytes 2097152 | tf_op jit(solution)/shard_map/all_to_all | solution.py:1930
  851.1 15.9 %copy-start.29 = (bf16[2048,704]{1,0:T(8,128)(2,1)S(1)}, bf16[2048,704]{1,0:T(8,128)(2,1)}, u32[]{:S(2)}) copy-start(bf16[2048,704]{1,0:T(8,128)(2,1)} %get-tuple-element.128) | copy-start | bytes 8650756
  867.0 10.3 %copy-start.31 = (bf16[2048,704]{1,0:T(8,128)(2,1)S(1)}, bf16[2048,704]{1,0:T(8,128)(2,1)}, u32[]{:S(2)}) copy-start(bf16[2048,704]{1,0:T(8,128)(2,1)} %get-tuple-element.127) | copy-start | bytes 8650756
  867.0 22.3 %slice-start = ((s8[8388608]{0:T(1024)(128)(4,1)}), s8[4194304]{0:T(1024)(128)(4,1)S(1)}, s32[]{:S(2)}) async-start(s8[8388608]{0:T(1024)(128)(4,1)} %bitcast.114), calls=%async_computation.6 | async-start | bytes 8388608
  877.3 12.0 %slice-start.1 = ((s8[8388608]{0:T(1024)(128)(4,1)}), s8[4194304]{0:T(1024)(128)(4,1)S(1)}, s32[]{:S(2)}) async-start(s8[8388608]{0:T(1024)(128)(4,1)} %bitcast.114), calls=%async_computation.7 | async-start | bytes 8388608
  877.3 12.0 %copy-start.30 = (bf16[2048,704]{1,0:T(8,128)(2,1)S(1)}, bf16[2048,704]{1,0:T(8,128)(2,1)}, u32[]{:S(2)}) copy-start(bf16[2048,704]{1,0:T(8,128)(2,1)} %get-tuple-element.126) | copy-start | bytes 8650756
  898.8 3.5 copy-start.3
Sparse Core Ops, SparseCore 0:
  11.5 155.5 all-gather.2
  261.9 80.0 all-gather.4
  466.1 273.4 reduce-scatter.1

commit v2 on v1

--- a/solution.py
+++ b/solution.py
@@ -1825,7 +1825,6 @@
         cosines,
         sines,
     )
-    head_rows, shared_in = lax.optimization_barrier((head_rows, shared_in))
     heads = exchange(head_rows.reshape(experts, rows, VALUE_UNITS), 1)
     heads = heads.transpose(1, 0, 2).reshape(rows, experts * VALUE_UNITS)
     half_heads = w_out.shape[0]
@@ -1836,6 +1835,7 @@
     normed_ffn = normed2.astype(jnp.bfloat16)
     router = jax.nn.softmax(outer_product(normed_ffn, wrout), axis=-1)
 
+    normed_ffn, shared_in = lax.optimization_barrier((normed_ffn, shared_in))
     (all_normed,) = gather_rows([normed_ffn], True, 2)
     w_query, all_normed = lax.optimization_barrier((w_query, all_normed))
     query_own, query_other = by_cores(w_query)
@@ -1864,13 +1864,6 @@
     g_gate = inner(d_pre_gate, ex_rows).T
     g_up = inner(d_pre_up, ex_rows).T
     (d_back,) = scatter_rows(d_part, True, 3)
-    out_part, d_back = lax.optimization_barrier((out_part, d_back))
-    out_sum = lax.psum_scatter(
-        out_part.reshape(blocks * rows, MODEL_WIDTH),
-        ("fsdp", "expert"),
-        scatter_dimension=0,
-        tiled=True,
-    )
     spare = router_rows.shape[0]
     d_hidden, d_attn, d_heads, g_router, g_ffn_grad = hidden_back(
         d_back,
@@ -1885,6 +1878,13 @@
     )
     g_router = g_router[:experts]
     d_head = exchange(d_heads, 4).reshape(seq_len, VALUE_UNITS)
+    out_part, d_head = lax.optimization_barrier((out_part, d_head))
+    out_sum = lax.psum_scatter(
+        out_part.reshape(blocks * rows, MODEL_WIDTH),
+        ("fsdp", "expert"),
+        scatter_dimension=0,
+        tiled=True,
+    )
     out_grad_part = inner(heads, d_attn).astype(jnp.bfloat16)
     d_query_full, d_pairs, d_keys = attend_back(
         query, key, value, d_head, head_sum, logs, expand_head, cosines, sines

time: 915 us -> 943 us (1.031)
  Pallas kernels: 771 us -> 802 us
    pallas_call x1, Pallas kernels: 120 us -> 149 us  [gather_and_scatter(): pl.pallas_call(functools.partial(gather_scatter_kernel, count, gated), ou...]
  transfers between devices with their start and end apart: 6 -> 6, of which waited for: 1 -> 0; matrix products, arithmetic and copies ran while one was open for 11% -> 11% of each run, Pallas kernels for 85% -> 85%
where the time goes in v2:
time: 943 us; the launch traced here: 939 us
  Pallas kernels  802 us (85%)
  matrix products  47.6 us (5%)
  local copies, waits for them, and re-layouts  35.2 us (4%)
  other arithmetic  29.1 us (3%)
  between operations  14.7 us (2%)
  starting transfers between devices  10.5 us (1%)
    pallas_call x3, Pallas kernels, gather_rows(): pl.pallas_call(functools.partial(gather_kernel, full, count, pairs, share...  204 us
    pallas_call x1, Pallas kernels, gather_and_scatter(): pl.pallas_call(functools.partial(gather_scatter_kernel, count, gated), ou...  149 us
    pallas_call x1, Pallas kernels, exchange_and_sums(): pl.pallas_call(functools.partial(sums_kernel, pairs), out_shape=[jax.Shap...  127 us
    pallas_call x1, Pallas kernels, expert_phase(): pl.pallas_call(functools.partial(expert_kernel, capacity), grid=(blocks /...  105 us
    pallas_call x1, Pallas kernels, scatter_rows(): pl.pallas_call(functools.partial(scatter_kernel, full, pairs), out_shape=...  97.7 us
    dot_general x6, matrix products, inner(): lax.dot_general(left, right, (((0,), (0,)), ((), ())), preferred_element_...  42.5 us
    pallas_call x2, Pallas kernels, exchange(): pl.pallas_call(exchange_kernel, out_shape=jax.ShapeDtypeStruct(x.shape, x...  38.5 us
    pallas_call x1, Pallas kernels, attend(): pl.pallas_call(attend_kernel, grid=(steps,), out_shape=[jax.ShapeDtypeStr...  24.9 us
  transfers between devices with their start and end apart: 6, of which 0 were waited for; matrix products, arithmetic and copies ran while one was open for 11% of the time, Pallas kernels for 85%

profile of v2, /device:TPU:0, one launch (start us, length us, event | category | flops | bytes accessed | tf_op | source)
XLA Modules:
  0.0 938.9 jit_solution(986790339001244471)
XLA Ops:
  8.1 1.9 fusion.8
  10.0 1.4 constant_dynamic-slice_fusion.6
  12.6 1.6 constant_dynamic-slice_fusion.5.refs_2_
  14.2 95.2 %shard_map.306 = (bf16[16,128,2048]{2,1,0:T(8,128)(2,1)}, bf16[224,1024]{1,0:T(8,128)(2,1)}, bf16[256,256]{1,0:T(8,128)(2,1)}, bf16[576,1024]{1,0:T(8,128)(2,1)}, bf16[1024,2048]{1,0:T(8,128)(2,1)}) custom-call(bf16[128,2048]{1,0:T(8,128)(2,1)} %bitcast.86, bf16[224,1024]{1,0:T(8,128)(2,1)} %pad.42.refs_1_, ...), custom_call_target="tpu_custom_call" | custom-call | bytes 100663296 | tf_op jit(solution)/shard_map/pallas_call | solution.py:687
  110.1 1.3 pad_maximum_fusion.3
  111.4 5.3 all-to-all-start
  117.0 1.2 broadcast_select_fusion.3
  121.2 1.4 broadcast_select_fusion.1
  122.7 2.0 pad_maximum_fusion.1.w_front
  124.7 24.9 %shard_map.307 = (bf16[2048,2048]{1,0:T(8,128)(2,1)}, bf16[2048,512]{1,0:T(8,128)(2,1)}, bf16[2048,192]{1,0:T(8,128)(2,1)}, bf16[2048,192]{1,0:T(8,128)(2,1)}, b...) custom-call(bf16[2048,2048]{1,0:T(8,128)(2,1)} %bitcast.109, ...), custom_call_target="tpu_custom_call" | custom-call | flops 8053063680 | bytes 25165824 | tf_op jit(solution)/shard_map/pallas_call | solution.py:1351
  149.6 16.9 %shard_map.308 = bf16[16,128,128]{2,1,0:T(8,128)(2,1)} custom-call(bf16[16,128,128]{2,1,0:T(8,128)(2,1)} %bitcast.101), custom_call_target="tpu_custom_call" | custom-call | bytes 10485760 | tf_op jit(solution)/shard_map/pallas_call | solution.py:1156
  166.5 1.3 copy.51
  167.9 3.2 convolution_add_fusion.1
  171.8 1.8 multiply_reduce_fusion
  174.7 2.2 copy.54
  176.9 1.5 pad_bitcast_fusion
  179.5 1.1 copy.64
  180.7 81.8 %shard_map.309.normed = bf16[32,128,2048]{2,1,0:T(8,128)(2,1)} custom-call(bf16[128,2048]{1,0:T(8,128)(2,1)} %multiply_convert_fusion.refs_0_.normed), custom_call_target="tpu_custom_call" | custom-call | bytes 201326592 | tf_op jit(solution)/shard_map/pallas_call | solution.py:687
  262.5 3.8 constant_dynamic-slice_fusion.2
  270.1 104.9 %shard_map.310 = (bf16[32,128,2048]{2,1,0:T(8,128)(2,1)}, bf16[32,128,2176]{2,1,0:T(8,128)(2,1)}, bf16[2048,2048]{1,0:T(8,128)(2,1)}, bf16[2048,2048]{1,0:T(8,12...) custom-call(bf16[32,128,2048]{2,1,0:T(8,128)(2,1)} %shard_map.309.no, ...), custom_call_target="tpu_custom_call" | custom-call | flops 35433480192 | bytes 167772160 | tf_op jit(solution)/shard_map/pallas_call | solution.py:1078
  375.0 97.7 %shard_map.311.d_back = f32[128,2176]{1,0:T(8,128)} custom-call(bf16[32,128,2176]{2,1,0:T(8,128)(2,1)} %get-tuple-element.89.part), custom_call_target="tpu_custom_call" | custom-call | bytes 213909504 | tf_op jit(solution)/shard_map/pallas_call | solution.py:919
  472.7 8.8 shard_map.312
  481.5 21.5 %shard_map.313 = bf16[16,128,128]{2,1,0:T(8,128)(2,1)} custom-call(bf16[16,128,128]{2,1,0:T(8,128)(2,1)} %get-tuple-element.90.x), custom_call_target="tpu_custom_call" | custom-call | bytes 10485760 | tf_op jit(solution)/shard_map/pallas_call | solution.py:1156
  504.0 1.5 constant_dynamic-slice_fusion
  505.5 1.6 pad_maximum_fusion.2.w_latent
  508.1 19.1 %shard_map.314 = (bf16[2048,192]{1,0:T(8,128)(2,1)}, bf16[2048,256]{1,0:T(8,128)(2,1)}, bf16[2048,640]{1,0:T(8,128)(2,1)}) custom-call(bf16[2048,192]{1,0:T(8,128)(2,1)} %get-tuple-element.80.query, bf16[2048,192]{1,0:T(8,128)(2,1)} %get-tuple-element.81.key, bf16[2048,128]{1,0:T(8,128)(2,1)} %get-tuple-element.82.value, bf16[2048,128]{1,0:T(8,128)(2,1)} %bitcast.100, ...), custom_call_target="tpu_custom_call" | custom-call | flops 4026531840 | bytes 6291456 | tf_op jit(solution)/shard_map/pallas_call | solution.py:1479
  527.2 2.1 convolution_convert_fusion.2
  529.9 5.4 convolution_convert_fusion.1
  536.2 5.7 convolution_convert_fusion
  541.9 127.4 %shard_map.315 = (bf16[16,128,192]{2,1,0:T(8,128)(2,1)}, f32[128,640]{1,0:T(8,128)}, f32[64,2048]{1,0:T(8,128)}, bf16[192,1024]{1,0:T(8,128)(2,1)}, bf16[256,256]{1,0:T(8,128)(2,1)}) custom-call(bf16[16,128,192]{2,1,0:T(8,128)(2,1)} %bitcast.81, bf16[16,128,640]{2,1,0:T(8,128)(2,1)} %bitcast.93, bf16[32,64,2048]{2,1,0:T(8,128)(2,1)} %bitcast.77, ...), custom_call_target="tpu_custom_call" | custom-call | bytes 100663296 | tf_op jit(solution)/shard_map/pallas_call | solution.py:1236
  669.3 13.8 %shard_map.316 = (bf16[128,2048]{1,0:T(8,128)(2,1)}, f32[576,2048]{1,0:T(8,128)}, f32[1,2048]{1,0:T(1,128)}, f32[1,512]{1,0:T(1,128)}) custom-call(bf16[16,128,192]{2,1,0:T(8,128)(2,1)} %get-tuple-element.103.d_query, f32[128,640]{1,0:T(8,128)} %get-tuple-element.104.d_sums, bf16[1024,3072]{1,0:T(8,128)(2,1)} %all-gather.5.cloned.1.call-done.query_own, ...), custom_call_target="tpu_custom_call" | custom-call | flops 1610612736 | bytes 16777216 | tf_op jit(solution)/shard_map/pallas_call | solution.py:1630
  684.6 2.7 maximum_convert_fusion
  688.1 2.4 pad_maximum_fusion.refs_3_
  692.1 148.6 %shard_map.317 = (bf16[16,192,1024]{2,1,0:T(8,128)(2,1)}, bf16[16,256,256]{2,1,0:T(8,128)(2,1)}, bf16[16,64,2048]{2,1,0:T(8,128)(2,1)}, f32[64,1024]{1,0:T(8,128)}) custom-call(bf16[192,1024]{1,0:T(8,128)(2,1)} %add_convert_fusion.1.refs_0_, bf16[256,256]{1,0:T(8,128)(2,1)} %add_convert_fusion.2.refs_1_, bf16[64,2048]{1,0:T(8,128)(2,1)} %convert_element_type.108.refs_2_, ...), custom_call_target="tpu_custom_call" | custom-call | bytes 150994944 | tf_op jit(solution)/shard_map/pallas_call | solution.py:896
  840.6 1.6 convert_element_type.111.refs_0_
  842.2 26.7 %shard_map.318 = bf16[16,64,1024]{2,1,0:T(8,128)(2,1)} custom-call(bf16[64,1024]{1,0:T(8,128)(2,1)} %convert_element_type.111.refs_0_), custom_call_target="tpu_custom_call" | custom-call | bytes 25165824 | tf_op jit(solution)/shard_map/pallas_call | solution.py:687
  868.9 2.2 convert_element_type.112
  871.2 1.7 slice.108
  874.5 3.6 all-to-all-start.1
  879.0 14.4 %shard_map.319 = (f32[1024,3072]{1,0:T(8,128)}, f32[256,4096]{1,0:T(8,128)}, f32[1024,2048]{1,0:T(8,128)}) custom-call(bf16[16,192,1024]{2,1,0:T(8,128)(2,1)} %get-tuple-element.117.query, bf16[16,256,256]{2,1,0:T(8,128)(2,1)} %get-tuple-element.118.expand, bf16[16,64,2048]{2,1,0:T(8,128)(2,1)} %get-tuple-element.119.out_rows), custom_call_target="tpu_custom_call" | custom-call | bytes 18874368 | tf_op jit(solution)/shard_map/pallas_call | solution.py:1672
  893.4 1.5 slice_bitcast_fusion
  894.9 10.3 %convolution_bitcast_fusion = f32[1,704,2048]{2,1,0:T(8,128)} fusion(bf16[2048,704]{1,0:T(8,128)(2,1)S(1)} %copy-done.29, bf16[2048,2048]{1,0:T(8,128)(2,1)} %get-tuple-element.129), kind=kOutput, calls=%fused_computation.8 | convolution fusion | flops 5905580032 | bytes 17039360 | tf_op jit(solution)/shard_map/dot_general | solution.py:28
  905.2 10.5 %convolution_bitcast_fusion.1 = f32[1,2048,704]{1,2,0:T(8,128)} fusion(bf16[2048,2048]{1,0:T(8,128)(2,1)} %get-tuple-element.125, bf16[2048,704]{1,0:T(8,128)(2,1)S(1)} %copy-done.31), kind=kOutput, calls=%fused_computation.9 | convolution fusion | flops 5905580032 | bytes 17039360 | tf_op jit(solution)/shard_map/dot_general | solution.py:28
  915.7 1.4 fusion.22
  917.2 8.5 convolution_bitcast_fusion.2
  926.7 1.4 reshape.134
  928.7 1.4 reshape.135
  930.2 1.9 fusion.9
  (131 shorter events, 24.0 us)
Async XLA Ops:
  7.2 4.4 copy-start.28
  7.2 4.4 copy-start.26
  7.2 4.4 copy-start.27
  7.2 4.4 copy-start.24
  7.2 262.9 %all-gather.3.cloned.1.call-start = ((), (), s32[]{:S(2)}) async-start(), calls=%async_computation.3 | async-start | bytes 18382848 | tf_op jit(solution)/shard_map/all_gather | solution.py:1698
  14.2 95.2 %copy-start.18 = (bf16[64,2816]{1,0:T(8,128)(2,1)S(1)}, bf16[64,2816]{1,0:T(8,128)(2,1)}, u32[]{:S(2)}) copy-start(bf16[64,2816]{1,0:T(8,128)(2,1)} %param.30) | copy-start | bytes 1081348
  14.2 95.6 %copy-start.19 = (bf16[64,2816]{1,0:T(8,128)(2,1)S(1)}, bf16[64,2816]{1,0:T(8,128)(2,1)}, u32[]{:S(2)}) copy-start(bf16[64,2816]{1,0:T(8,128)(2,1)} %param.31) | copy-start | bytes 1081348
  109.7 9.1 copy-start.22
  111.4 9.8 %copy-start.10 = (bf16[1024,576]{0,1:T(8,128)(2,1)S(1)}, bf16[1024,576]{0,1:T(8,128)(2,1)}, u32[]{:S(2)}) copy-start(bf16[1024,576]{0,1:T(8,128)(2,1)} %param.24) | copy-start | bytes 3538948
  111.4 63.3 %all-to-all-start = ((bf16[32,128,88]{1,2,0:T(8,128)(2,1)}), bf16[32,128,88]{1,2,0:T(8,128)(2,1)}, u32[]{:S(2)}, u32[]{:S(2)}) async-start(bf16[32,128,88]{1,2,0:T(8,128)(2,1)} %bitcast.10), calls=%async_computation | async-start | bytes 1441792 | tf_op jit(solution)/shard_map/all_to_all | solution.py:1787
  116.7 386.4 %all-gather.5.cloned.1.call-start = ((), (), s32[]{:S(2)}) async-start(), calls=%async_computation.4 | async-start | bytes 9437184 | tf_op jit(solution)/shard_map/all_gather | solution.py:1774
  121.1 52.5 %copy-start.23 = (f32[1,2048]{1,0:T(1,128)}, f32[1,2048]{1,0:T(1,128)S(1)}, u32[]{:S(2)}) copy-start(f32[1,2048]{1,0:T(1,128)S(1)} %get-tuple-element.140.gain) | copy-start | bytes 24580
  122.6 2.1 copy-start.4
  124.7 43.2 %copy-start.11 = (bf16[1,128,2048]{2,1,0:T(8,128)(2,1)S(1)}, bf16[1,128,2048]{2,1,0:T(8,128)(2,1)}, u32[]{:S(2)}) copy-start(bf16[1,128,2048]{2,1,0:T(8,128)(2,1)} %param.19) | copy-start | bytes 1572868
  167.8 3.2 copy-start.8
  167.9 3.9 copy-start.1
  173.6 6.0 copy-start.2
  266.3 1.0 copy-start.20
  266.3 1.8 copy-start.6
  266.3 663.9 %reduce-scatter.2.cloned.1.call-start = ((), (), s32[]{:S(2)}) async-start(), calls=%async_computation.5 | async-start | bytes 17301504 | tf_op jit(solution)/shard_map/reduce_scatter | solution.py:1882
  503.1 2.5 copy-start.5
  503.1 166.1 %collective-permute-start = (bf16[1024,3072]{1,0:T(8,128)(2,1)}, bf16[1024,3072]{1,0:T(8,128)(2,1)}, u32[]{:S(2)}, u32[]{:S(2)}) collective-permute-start(bf16[1024,3072]{1,0:T(8,128)(2,1)} %all-gather.5.cloned.1.call-done.query_own), channel_id=1, source_target_pairs={{0,2},{2,0},{4,6},{6,4},{8,10},{10,8},{12,14},{14,12},{16,18},{18,... | collective-permute-start | bytes 18874376 | tf_op jit(solution)/shard_map/ppermute | solution.py:1776
  508.1 19.1 %copy-start.13 = (bf16[2048,512]{1,0:T(8,128)(2,1)S(1)}, bf16[2048,512]{1,0:T(8,128)(2,1)}, u32[]{:S(2)}) copy-start(bf16[2048,512]{1,0:T(8,128)(2,1)} %get-tuple-element.98) | copy-start | bytes 6291460
  527.2 2.8 copy-start.7
  529.9 6.2 copy-start.9
  529.9 6.2 copy-start.15
  669.3 14.6 %copy-start.14 = (f32[64,2048]{1,0:T(8,128)S(1)}, f32[64,2048]{1,0:T(8,128)}, u32[]{:S(2)}) copy-start(f32[64,2048]{1,0:T(8,128)} %get-tuple-element.102) | copy-start | bytes 1572868
  669.3 15.3 %copy-start.25 = (f32[1,2048]{1,0:T(1,128)S(1)}, f32[1,2048]{1,0:T(1,128)}, u32[]{:S(2)}) copy-start(f32[1,2048]{1,0:T(1,128)} %get-tuple-element.110) | copy-start | bytes 24580
  688.1 2.4 copy-start.21
  688.1 3.1 copy-start.17
  868.9 2.2 copy-start
  871.2 2.7 copy-start.12
  871.2 6.9 copy-start.16
  874.5 51.2 %all-to-all-start.1 = ((bf16[32,64,256]{2,1,0:T(8,128)(2,1)}), bf16[32,64,256]{2,1,0:T(8,128)(2,1)S(1)}, u32[]{:S(2)}, u32[]{:S(2)}) async-start(bf16[32,64,256]{2,1,0:T(8,128)(2,1)} %bitcast.37), calls=%async_computation.2 | async-start | bytes 2097152 | tf_op jit(solution)/shard_map/all_to_all | solution.py:1930
  879.0 15.9 %copy-start.29 = (bf16[2048,704]{1,0:T(8,128)(2,1)S(1)}, bf16[2048,704]{1,0:T(8,128)(2,1)}, u32[]{:S(2)}) copy-start(bf16[2048,704]{1,0:T(8,128)(2,1)} %get-tuple-element.128) | copy-start | bytes 8650756
  894.9 10.3 %copy-start.31 = (bf16[2048,704]{1,0:T(8,128)(2,1)S(1)}, bf16[2048,704]{1,0:T(8,128)(2,1)}, u32[]{:S(2)}) copy-start(bf16[2048,704]{1,0:T(8,128)(2,1)} %get-tuple-element.127) | copy-start | bytes 8650756
  894.9 22.3 %slice-start = ((s8[8388608]{0:T(1024)(128)(4,1)}), s8[4194304]{0:T(1024)(128)(4,1)S(1)}, s32[]{:S(2)}) async-start(s8[8388608]{0:T(1024)(128)(4,1)} %bitcast.114), calls=%async_computation.6 | async-start | bytes 8388608
  905.2 12.0 %slice-start.1 = ((s8[8388608]{0:T(1024)(128)(4,1)}), s8[4194304]{0:T(1024)(128)(4,1)S(1)}, s32[]{:S(2)}) async-start(s8[8388608]{0:T(1024)(128)(4,1)} %bitcast.114), calls=%async_computation.7 | async-start | bytes 8388608
  905.2 12.0 %copy-start.30 = (bf16[2048,704]{1,0:T(8,128)(2,1)S(1)}, bf16[2048,704]{1,0:T(8,128)(2,1)}, u32[]{:S(2)}) copy-start(bf16[2048,704]{1,0:T(8,128)(2,1)} %get-tuple-element.126) | copy-start | bytes 8650756
  926.7 3.5 copy-start.3
Sparse Core Ops, SparseCore 0:
  11.5 166.8 all-gather.2
  266.4 80.6 all-gather.4
  503.2 291.4 reduce-scatter.1
